TPU v7x, 128 devices: a whole 4x4x4 slice. The times are simulated.
128 devices in a mesh: group: 32 (over x_lo, y, z), tensor: 4 (over x_hi, core).
Axes of the slice: x: 4 (x_hi: 2, x_lo: 2; x = x_hi * 2 + x_lo), y: 4, z: 4, core: 2. Of those that a mesh axis runs over, the one named last changes fastest.
Arguments:
- layer_in: bfloat16 [4, 1024, 4096], P(None, 'group'), may hold values from -6 to 6
- lengths: int32 [1024], P('group'), may hold values from 1 to 4
- prior_state: bfloat16 [1024, 64, 64, 256], P('group', 'tensor'), may hold values from -6 to 6
- weight_x: bfloat16 [4096, 4096], P(('group', 'tensor')), may hold values from -0.09375 to 0.09375
- weight_z: bfloat16 [4096, 4096], P(('group', 'tensor')), may hold values from -0.09375 to 0.09375
- weight_b: bfloat16 [4096, 1024], P(('group', 'tensor')), may hold values from -0.09375 to 0.09375
- weight_c: bfloat16 [4096, 1024], P(('group', 'tensor')), may hold values from -0.09375 to 0.09375
- weight_step: bfloat16 [4096, 64], P(('group', 'tensor')), may hold values from -0.09375 to 0.09375
- weight_out: bfloat16 [4096, 4096], P(None, ('group', 'tensor')), may hold values from -0.09375 to 0.09375
- log_rate: float32 [64], P('tensor'), may hold values from -1 to 1.5
- step_bias: float32 [64], P('tensor'), may hold values from -4 to -1
- skip_gain: float32 [64], P('tensor'), may hold values from 1 to 4
- norm_gain: float32 [4096], P('tensor'), may hold values from 0.1 to 1.9
Outputs:
- layer_out: bfloat16 [4, 1024, 4096], P(None, 'group', 'tensor')
All inputs are finite; a program needn't handle non-finite values.
Results may differ from a plain program's by a relative error of at most 0.0033.
Values may be sent and summed in bfloat16 or wider, within the bound.
A program may use at most 128 MiB of HBM per device.

v0:
```python
import jax
import jax.numpy as jnp
from jax import lax
from jax.sharding import PartitionSpec as P

eps = 1e-05


def shards(
    layer_in,
    lengths,
    prior_state,
    weight_x,
    weight_z,
    weight_b,
    weight_c,
    weight_step,
    weight_out,
    log_rate,
    step_bias,
    skip_gain,
    norm_gain,
):
    tensor_count = lax.axis_size("tensor")
    step_count, row_count, model_width = layer_in.shape
    flat_in = layer_in.reshape(step_count * row_count, model_width)
    parted = (
        lax.all_to_all(weight_x, "tensor", split_axis=1, concat_axis=0, tiled=True),
        lax.all_to_all(weight_z, "tensor", split_axis=1, concat_axis=0, tiled=True),
        lax.all_to_all(weight_b, "tensor", split_axis=1, concat_axis=0, tiled=True),
        lax.all_to_all(weight_c, "tensor", split_axis=1, concat_axis=0, tiled=True),
        lax.all_to_all(weight_step, "tensor", split_axis=1, concat_axis=0, tiled=True),
    )
    gathered = (
        lax.all_gather(parted[0], "group", axis=0, tiled=True),
        lax.all_gather(parted[1], "group", axis=0, tiled=True),
        lax.all_gather(parted[2], "group", axis=0, tiled=True),
        lax.all_gather(parted[3], "group", axis=0, tiled=True),
        lax.all_gather(parted[4], "group", axis=0, tiled=True),
    )
    flat_proj = tuple(
        (jnp.dot(flat_in, member, preferred_element_type=jnp.float32) for member in gathered)
    )
    out_part = lax.all_to_all(weight_out, "tensor", split_axis=0, concat_axis=1, tiled=True)
    out_full = lax.all_gather(out_part, "group", axis=1, tiled=True)
    x_all, z_all, b_all, c_all, d_all = tuple(
        (member.reshape(step_count, row_count, member.shape[1]) for member in flat_proj)
    )
    heads_here = log_rate.shape[0]
    head_size = x_all.shape[2] // heads_here
    base_rate = jnp.exp(log_rate)
    carried = prior_state.astype(jnp.float32)
    col_count = model_width // tensor_count
    col_start = lax.axis_index("tensor") * col_count
    residual_all = lax.dynamic_slice_in_dim(layer_in, col_start, col_count, 2).astype(jnp.float32)
    partial_list = []
    for position in range(step_count):
        active = lengths > position
        step_size = jax.nn.softplus(d_all[position] + step_bias)
        decay_rate = jnp.exp(-base_rate * step_size)
        x_heads = x_all[position].reshape(row_count, heads_here, head_size)
        drive_term = (step_size[:, :, None] * x_heads)[..., None] * b_all[position][
            :, None, None, :
        ]
        updated = decay_rate[:, :, None, None] * carried + drive_term
        carried = jnp.where(active[:, None, None, None], updated, carried)
        mixed_y = (
            jnp.einsum("rhpn,rn->rhp", carried, c_all[position], precision=lax.Precision.HIGHEST)
            + skip_gain[:, None] * x_heads
        )
        gated_out = mixed_y.reshape(row_count, heads_here * head_size) * jax.nn.silu(
            z_all[position]
        )
        inv_rms = lax.rsqrt(jnp.mean(gated_out * gated_out, axis=1, keepdims=True) + eps)
        hidden = (gated_out * inv_rms * norm_gain).astype(jnp.bfloat16)
        partials = jnp.dot(hidden, out_full, preferred_element_type=jnp.float32)
        partial_list.append(lax.psum_scatter(partials, "tensor", scatter_dimension=1, tiled=True))
    mixed_out = jnp.stack(partial_list)
    active_all = lengths[None, :] > jnp.arange(step_count, dtype=jnp.int32)[:, None]
    return jnp.where(active_all[:, :, None], residual_all + mixed_out, residual_all).astype(
        jnp.bfloat16
    )


def solution(mesh):
    placed = (
        P(None, "group", None),
        P("group"),
        P("group", "tensor", None, None),
        P(("group", "tensor"), None),
        P(("group", "tensor"), None),
        P(("group", "tensor"), None),
        P(("group", "tensor"), None),
        P(("group", "tensor"), None),
        P(None, ("group", "tensor")),
        P("tensor"),
        P("tensor"),
        P("tensor"),
        P("tensor"),
    )
    return jax.shard_map(
        shards, mesh=mesh, in_specs=placed, out_specs=P(None, "group", "tensor"), check_vma=False
    )
```

profile of v0, /device:TPU:1, one launch (start us, length us, event | category | flops | bytes accessed | tf_op | source)
XLA Modules:
  0.0 973.0 jit_solution(12841853409192675536)
XLA Ops:
  6.5 0.8 copy.95
  7.4 10.5 %all_to_all.114 = bf16[32,4,256]{2,0,1:T(8,128)(2,1)} all-to-all(bf16[32,4,256]{2,0,1:T(8,128)(2,1)S(1)} %bitcast.93), channel_id=1, replica_groups=mesh['group'=32,'tensor'=4] {'tensor'}, dimensions={1} | all-to-all | bytes 131072 | tf_op jit(solution)/shard_map/all_to_all | solution.py:30
  17.9 0.8 copy.94
  18.8 8.7 all_to_all.115
  27.5 1.0 copy.93
  28.5 11.5 %all_to_all.116 = bf16[32,4,1024]{2,0,1:T(8,128)(2,1)} all-to-all(bf16[32,4,1024]{2,0,1:T(8,128)(2,1)S(1)} %bitcast.86), channel_id=1, replica_groups=mesh['group'=32,'tensor'=4] {'tensor'}, dimensions={1} | all-to-all | bytes 524288 | tf_op jit(solution)/shard_map/all_to_all | solution.py:28
  40.0 1.0 copy.92
  41.0 11.1 %all_to_all.117 = bf16[32,4,1024]{2,0,1:T(8,128)(2,1)} all-to-all(bf16[32,4,1024]{2,0,1:T(8,128)(2,1)S(1)} %bitcast.87), channel_id=1, replica_groups=mesh['group'=32,'tensor'=4] {'tensor'}, dimensions={1} | all-to-all | bytes 524288 | tf_op jit(solution)/shard_map/all_to_all | solution.py:29
  52.1 0.8 copy.47
  52.9 0.7 reshape.319
  53.6 4.3 all-to-all-start
  57.9 0.7 broadcast_compare_fusion.2
  58.6 0.7 exponential_negate_fusion
  59.2 1.7 copy.91
  60.9 1.6 all-to-all-done
  62.5 4.1 all-to-all-start.5
  66.8 70.2 %all_gather.18 = bf16[4096,16]{0,1:T(8,128)(2,1)S(1)} all-gather(bf16[128,16]{0,1:T(8,128)(2,1)S(1)} %all_to_all.87), channel_id=1, replica_groups=mesh['group'=32,'tensor'=4] {'group'}, dimensions={0}, use_global_device_ids=true | all-gather | bytes 135168 | tf_op jit(solution)/shard_map/all_gather | solution.py:39
  137.0 1.6 fusion.68
  138.6 0.8 multiply_exponential_fusion.2
  140.0 0.7 copy-done.9
  140.7 10.8 %all-gather.8.cloned.1.call-done = bf16[4096,256]{1,0:T(8,128)(2,1)} async-done(((bf16[128,256]{1,0:T(8,128)(2,1)}), bf16[4096,256]{1,0:T(8,128)(2,1)}) %all-gather.8.cloned.1.call-update) | async-done | bytes 2097168 | tf_op jit(solution)/shard_map/all_gather | solution.py:37
  151.5 2.4 fusion.70
  153.9 152.7 %all-gather.10.cloned.1.call-done = bf16[4096,256]{1,0:T(8,128)(2,1)} async-done(((bf16[128,256]{1,0:T(8,128)(2,1)}), bf16[4096,256]{1,0:T(8,128)(2,1)}) %all-gather.10.cloned.1.call-update) | async-done | bytes 2097168 | tf_op jit(solution)/shard_map/all_gather | solution.py:38
  306.6 2.4 fusion.71
  309.0 169.2 %all-gather.6.cloned.1.call-done = bf16[4096,1024]{1,0:T(8,128)(2,1)} async-done(((bf16[128,1024]{1,0:T(8,128)(2,1)}), bf16[4096,1024]{1,0:T(8,128)(2,1)}) %all-gather.6.cloned.1.call-update) | async-done | bytes 8388624 | tf_op jit(solution)/shard_map/all_gather | solution.py:35
  478.2 5.0 fusion.69
  483.7 0.2 broadcast_multiply_fusion.2
  483.9 0.2 broadcast_multiply_fusion
  484.1 48.2 %fusion.6 = f32[32,1,16,64]{3,1,2,0:T(1,128)S(1)} fusion(bf16[32,16,64,256]{3,2,1,0:T(8,128)(2,1)} %param.15, f32[32,256]{1,0:T(8,128)S(1)} %get-tuple-element.28, f32[32,16,64]{2,1,0:T(8,128)S(1)} %get-tuple-element.44, f32[32,16]{1,0:T(8,128)S(1)} %copy.49, pred[32]{0:T(512)(128)(4,1)S(1)} %get-tuple-element.40, f32[32,256,1,1]{1,0,2,3:T(8,128)S(1)} %get-tuple-element.24), kind=kOutput, calls=%fused_computation.10 | convolution fusion | flops 142606336 | bytes 17106976 | tf_op jit(solution)/shard_map/rhpn,rn->rhp/dot_general | solution.py:68
  532.4 55.2 %fusion.7 = f32[32,1,16,64]{3,1,2,0:T(1,128)S(1)} fusion(bf16[32,16,64,256]{3,2,1,0:T(8,128)(2,1)S(1)} %bitcast.107, f32[32,256]{1,0:T(8,128)S(1)} %get-tuple-element.25, f32[32,16,64]{2,1,0:T(8,128)S(1)} %get-tuple-element.43, f32[32,16]{1,0:T(8,128)S(1)} %copy.56, f32[32,256]{1,0:T(8,128)S(1)} %get-tuple-element.28, ...), kind=kOutput, calls=%fused_computation.11 | convolution fusion | flops 176160768 | bytes 17272896 | tf_op jit(solution)/shard_map/rhpn,rn->rhp/dot_general | solution.py:68
  587.5 60.4 %fusion.8 = f32[32,1,16,64]{3,1,2,0:T(1,128)S(1)} fusion(bf16[32,16,64,256]{3,2,1,0:T(8,128)(2,1)S(1)} %bitcast.107, f32[32,256]{1,0:T(8,128)S(1)} %get-tuple-element.27, f32[32,16,64]{2,1,0:T(8,128)S(1)} %get-tuple-element.46, f32[32,16]{1,0:T(8,128)S(1)} %copy.58, f32[32,256]{1,0:T(8,128)S(1)} %get-tuple-element.25, ...), kind=kOutput, calls=%fused_computation.12 | convolution fusion | flops 209715200 | bytes 17438816 | tf_op jit(solution)/shard_map/rhpn,rn->rhp/dot_general | solution.py:68
  648.1 65.9 %fusion.1 = f32[32,1,16,64]{3,1,2,0:T(1,128)S(1)} fusion(bf16[32,16,64,256]{3,2,1,0:T(8,128)(2,1)S(1)} %bitcast.107, f32[32,256]{1,0:T(8,128)S(1)} %get-tuple-element.26, f32[32,16,64]{2,1,0:T(8,128)S(1)} %get-tuple-element.45, f32[32,16]{1,0:T(8,128)S(1)} %copy.60, f32[32,256]{1,0:T(8,128)S(1)} %get-tuple-element.27, ...), kind=kOutput, calls=%fused_computation.3 | convolution fusion | flops 243269632 | bytes 17604736 | tf_op jit(solution)/shard_map/rhpn,rn->rhp/dot_general | solution.py:68
  714.0 0.2 multiply_add_fusion.2
  714.2 0.1 reshape.307
  714.4 0.1 reshape.308
  714.5 0.1 reshape.309
  714.8 4.7 fusion.72
  719.4 0.3 multiply_reduce_fusion.3
  719.7 97.1 %all-gather.14.cloned.1.call-done = bf16[1024,4096]{0,1:T(8,128)(2,1)} async-done(((bf16[1024,128]{0,1:T(8,128)(2,1)}), bf16[1024,4096]{0,1:T(8,128)(2,1)}) %all-gather.14.cloned.1.call-update) | async-done | bytes 8388624 | tf_op jit(solution)/shard_map/all_gather | solution.py:45
  816.9 6.8 fusion.50
  823.7 6.7 fusion.51
  830.6 6.7 fusion.52
  837.4 6.8 fusion.53
  844.2 28.1 %reduce-scatter.5.cloned.1.call-done = f32[32,1024]{1,0:T(8,128)} async-done(((f32[32,4096]{1,0:T(8,128)}), f32[32,1024]{1,0:T(8,128)}) %reduce-scatter.5.cloned.1.call-update) | async-done | bytes 131088 | tf_op jit(solution)/shard_map/reduce_scatter | solution.py:77
  872.3 30.8 %reduce-scatter.7.cloned.1.call-done = f32[32,1024]{1,0:T(8,128)} async-done(((f32[32,4096]{1,0:T(8,128)}), f32[32,1024]{1,0:T(8,128)}) %reduce-scatter.7.cloned.1.call-update) | async-done | bytes 131088 | tf_op jit(solution)/shard_map/reduce_scatter | solution.py:77
  903.1 30.6 %reduce-scatter.9.cloned.1.call-done = f32[32,1024]{1,0:T(8,128)} async-done(((f32[32,4096]{1,0:T(8,128)}), f32[32,1024]{1,0:T(8,128)}) %reduce-scatter.9.cloned.1.call-update) | async-done | bytes 131088 | tf_op jit(solution)/shard_map/reduce_scatter | solution.py:77
  933.7 30.8 %reduce-scatter.11.cloned.1.call-done = f32[32,1024]{1,0:T(8,128)} async-done(((f32[32,4096]{1,0:T(8,128)}), f32[32,1024]{1,0:T(8,128)}) %reduce-scatter.11.cloned.1.call-update) | async-done | bytes 131088 | tf_op jit(solution)/shard_map/reduce_scatter | solution.py:77
  964.5 1.9 fusion.49
  (79 shorter events, 2.0 us)
Async XLA Ops:
  6.5 145.0 %all-gather.8.cloned.1.call-start = ((), (), s32[]{:S(2)}) async-start(), calls=%async_computation.11 | async-start | bytes 2162688 | tf_op jit(solution)/shard_map/all_gather | solution.py:37
  17.9 288.7 %all-gather.10.cloned.1.call-start = ((), (), s32[]{:S(2)}) async-start(), calls=%async_computation.12 | async-start | bytes 2162688 | tf_op jit(solution)/shard_map/all_gather | solution.py:38
  27.4 450.8 %all-gather.6.cloned.1.call-start = ((), (), s32[]{:S(2)}) async-start(), calls=%async_computation.10 | async-start | bytes 8650752 | tf_op jit(solution)/shard_map/all_gather | solution.py:35
  40.0 674.8 %all-gather.12.cloned.1.call-start = ((), (), s32[]{:S(2)}) async-start(), calls=%async_computation.13 | async-start | bytes 8650752 | tf_op jit(solution)/shard_map/all_gather | solution.py:36
  53.6 8.9 all-to-all-start
  62.5 77.4 %all-to-all-start.5 = ((bf16[4,1024,32]{1,2,0:T(8,128)(2,1)}), bf16[4,1024,32]{1,2,0:T(8,128)(2,1)S(1)}, u32[]{:S(2)}, u32[]{:S(2)}) async-start(bf16[4,1024,32]{1,2,0:T(8,128)(2,1)} %bitcast.73), calls=%async_computation.5 | async-start | bytes 524288 | tf_op jit(solution)/shard_map/all_to_all | solution.py:44
  66.6 750.3 %all-gather.14.cloned.1.call-start = ((), (), s32[]{:S(2)}) async-start(), calls=%async_computation.14 | async-start | bytes 8650752 | tf_op jit(solution)/shard_map/all_gather | solution.py:45
  140.0 0.7 copy-start.9
  140.7 731.6 %reduce-scatter.5.cloned.1.call-start = ((), (), s32[]{:S(2)}) async-start(), calls=%async_computation.15 | async-start | bytes 655360 | tf_op jit(solution)/shard_map/reduce_scatter | solution.py:77
  483.3 49.0 %copy-start.1 = (f32[32,16,64]{2,1,0:T(8,128)}, f32[32,16,64]{2,1,0:T(8,128)S(1)}, u32[]{:S(2)}) copy-start(f32[32,16,64]{2,1,0:T(8,128)S(1)} %reshape_squeeze.12) | copy-start | bytes 393220
  483.4 48.9 %copy-start.3 = (f32[32,16,64]{2,1,0:T(8,128)}, f32[32,16,64]{2,1,0:T(8,128)S(1)}, u32[]{:S(2)}) copy-start(f32[32,16,64]{2,1,0:T(8,128)S(1)} %reshape_squeeze.13) | copy-start | bytes 393220
  483.6 48.8 %copy-start.5 = (f32[32,16,64]{2,1,0:T(8,128)}, f32[32,16,64]{2,1,0:T(8,128)S(1)}, u32[]{:S(2)}) copy-start(f32[32,16,64]{2,1,0:T(8,128)S(1)} %reshape_squeeze.14) | copy-start | bytes 393220
  483.7 48.7 %copy-start.7 = (f32[32,16,64]{2,1,0:T(8,128)}, f32[32,16,64]{2,1,0:T(8,128)S(1)}, u32[]{:S(2)}) copy-start(f32[32,16,64]{2,1,0:T(8,128)S(1)} %reshape_squeeze.15) | copy-start | bytes 393220
  483.9 48.5 %slice-start = ((s8[16777216]{0:T(1024)(128)(4,1)}), s8[4194304]{0:T(1024)(128)(4,1)S(1)}, s32[]{:S(2)}) async-start(s8[16777216]{0:T(1024)(128)(4,1)} %bitcast.106), calls=%async_computation.19 | async-start | bytes 8388608
  484.1 48.3 %slice-start.1 = ((s8[16777216]{0:T(1024)(128)(4,1)}), s8[4194304]{0:T(1024)(128)(4,1)S(1)}, s32[]{:S(2)}) async-start(s8[16777216]{0:T(1024)(128)(4,1)} %bitcast.106), calls=%async_computation.20 | async-start | bytes 8388608
  484.1 48.3 %slice-start.2 = ((s8[16777216]{0:T(1024)(128)(4,1)}), s8[4194304]{0:T(1024)(128)(4,1)S(1)}, s32[]{:S(2)}) async-start(s8[16777216]{0:T(1024)(128)(4,1)} %bitcast.106), calls=%async_computation.21 | async-start | bytes 8388608
  484.1 48.3 %slice-start.3 = ((s8[16777216]{0:T(1024)(128)(4,1)}), s8[4194304]{0:T(1024)(128)(4,1)S(1)}, s32[]{:S(2)}) async-start(s8[16777216]{0:T(1024)(128)(4,1)} %bitcast.106), calls=%async_computation.22 | async-start | bytes 8388608
  648.0 66.0 %copy-start.2 = (f32[32,16,64]{2,1,0:T(8,128)S(1)}, f32[32,16,64]{2,1,0:T(8,128)}, u32[]{:S(2)}) copy-start(f32[32,16,64]{2,1,0:T(8,128)} %copy-done.1) | copy-start | bytes 393220
  648.0 66.0 %copy-start.4 = (f32[32,16,64]{2,1,0:T(8,128)S(1)}, f32[32,16,64]{2,1,0:T(8,128)}, u32[]{:S(2)}) copy-start(f32[32,16,64]{2,1,0:T(8,128)} %copy-done.3) | copy-start | bytes 393220
  648.0 66.0 %copy-start.6 = (f32[32,16,64]{2,1,0:T(8,128)S(1)}, f32[32,16,64]{2,1,0:T(8,128)}, u32[]{:S(2)}) copy-start(f32[32,16,64]{2,1,0:T(8,128)} %copy-done.5) | copy-start | bytes 393220
  648.0 66.0 %copy-start.8 = (f32[32,16,64]{2,1,0:T(8,128)S(1)}, f32[32,16,64]{2,1,0:T(8,128)}, u32[]{:S(2)}) copy-start(f32[32,16,64]{2,1,0:T(8,128)} %copy-done.7) | copy-start | bytes 393220
  648.0 66.0 %copy-start.12 = (f32[16]{0:T(128)S(1)}, f32[16]{0:T(128)}, u32[]{:S(2)}) copy-start(f32[16]{0:T(128)} %param.24) | copy-start | bytes 196
  648.0 66.7 %copy-start = (bf16[4,32,4096]{2,1,0:T(8,128)(2,1)S(1)}, bf16[4,32,4096]{2,1,0:T(8,128)(2,1)}, u32[]{:S(2)}) copy-start(bf16[4,32,4096]{2,1,0:T(8,128)(2,1)} %param.13) | copy-start | bytes 3145732
  713.9 102.9 %copy-start.10 = (f32[1024]{0:T(1024)S(1)}, f32[1024]{0:T(1024)}, u32[]{:S(2)}) copy-start(f32[1024]{0:T(1024)} %param.25) | copy-start | bytes 12292
  823.7 20.5 %copy-start.11 = (s32[32]{0:T(128)S(1)}, s32[32]{0:T(128)}, u32[]{:S(2)}) copy-start(s32[32]{0:T(128)} %param.14) | copy-start | bytes 388
  823.7 79.4 %reduce-scatter.7.cloned.1.call-start = ((), (), s32[]{:S(2)}) async-start(), calls=%async_computation.16 | async-start | bytes 655360 | tf_op jit(solution)/shard_map/reduce_scatter | solution.py:77
  830.5 103.2 %reduce-scatter.9.cloned.1.call-start = ((), (), s32[]{:S(2)}) async-start(), calls=%async_computation.17 | async-start | bytes 655360 | tf_op jit(solution)/shard_map/reduce_scatter | solution.py:77
  837.3 127.2 %reduce-scatter.11.cloned.1.call-start = ((), (), s32[]{:S(2)}) async-start(), calls=%async_computation.18 | async-start | bytes 655360 | tf_op jit(solution)/shard_map/reduce_scatter | solution.py:77
Sparse Core Ops, SparseCore 0:
  18.0 133.5 all-gather.7
  153.2 153.3 all-gather.9
  308.2 169.9 all-gather.5
  479.7 167.6 all-gather.11
  648.9 167.9 all-gather.13
  823.8 48.4 reduce-scatter.4
  875.1 27.9 reduce-scatter.6
  905.7 27.9 reduce-scatter.8
  936.5 27.9 reduce-scatter.10
where the time goes:
time: 974 us; the launch traced here: 973 us
  waiting for transfers between devices  552 us (57%)
  matrix products  273 us (28%)
  blocking collectives  112 us (11%)
  between operations  13.6 us (1%)
    dot_general x4, matrix products, shards(): jnp.einsum('rhpn,rn->rhp', carried, c_all[position], precision=lax.Precis...  230 us
    all_gather x1, waiting for transfers between devices, shards(): lax.all_gather(parted[0], 'group', axis=0, tiled=True)  169 us
    all_gather x1, waiting for transfers between devices, shards(): lax.all_gather(parted[3], 'group', axis=0, tiled=True)  153 us
    reduce_scatter x4, waiting for transfers between devices, shards(): lax.psum_scatter(partials, 'tensor', scatter_dimension=1, tiled=True)  120 us
    all_gather x1, waiting for transfers between devices, shards(): out_full = lax.all_gather(out_part, 'group', axis=1, tiled=True)  97.1 us
    all_gather x1, blocking collectives, shards(): lax.all_gather(parted[4], 'group', axis=0, tiled=True)  70.2 us
    dot_general x4, matrix products, shards(): partials = jnp.dot(hidden, out_full, preferred_element_type=jnp.float32)  27 us
  transfers between devices with their start and end apart: 11, of which 9 were waited for; matrix products, arithmetic and copies ran while one was open for 28% of the time, Pallas kernels for 0%

commit v1 on v0

v1 whole, which is shorter than its diff:
```python
import jax
import jax.numpy as jnp
from jax import lax
from jax.experimental import pallas as pl
from jax.experimental.pallas import tpu as pltpu
from jax.sharding import PartitionSpec as P

MESH = pl.DeviceIdType.MESH
eps = 1e-05


def here():
    group, tensor = lax.axis_index("group"), lax.axis_index("tensor")
    return (tensor // 2) * 2 + group // 16, (group // 4) % 4, group % 4, tensor % 2


def device(x, y, z, core):
    return ((x % 2) * 16 + (y % 4) * 4 + z % 4, ((x % 4) // 2) * 2 + core % 2)


def remote(source, target, send_sem, recv_sem, where):
    return pltpu.make_async_remote_copy(
        src_ref=source,
        dst_ref=target,
        send_sem=send_sem,
        recv_sem=recv_sem,
        device_id=where,
        device_id_type=MESH,
    )


def arrived(ref, sem):
    pltpu.make_async_copy(ref, ref, sem).wait()


def greet(partners, count):
    barrier = pltpu.get_barrier_semaphore()
    for partner in partners:
        pl.semaphore_signal(barrier, inc=1, device_id=partner, device_id_type=MESH)
    pl.semaphore_wait(barrier, count)


def project_kernel(
    pack_ref,
    fold_ref,
    act_ref,
    xz_ref,
    bc_ref,
    step_ref,
    act,
    weights,
    folded,
    keep,
    give,
    got,
    rounded,
    shared_sum,
    step_give,
    step_got,
    own_sem,
    f_send,
    f_recv,
    g_send,
    g_recv,
    t_sem,
    a_send,
    a_recv,
    b_send,
    b_recv,
    z_send,
    z_recv,
    x_send,
    x_recv,
    d_send,
    d_recv,
    r_send,
    r_recv,
    c_send,
    c_recv,
):
    x, y, z, core = here()
    x_lo, x_hi = x % 2, x // 2
    partners = [
        device(x + dx, y, z + dz, core + dc)
        for dx in range(4)
        for dz in range(4)
        for dc in range(2)
        if (dx, dz, dc) != (0, 0, 0)
    ]
    partners += [device(x, y + 1, z, core), device(x, y + 3, z, core)]
    greet(partners, len(partners))

    row = pl.multiple_of(y * 512 + z * 128 + x_hi * 64 + core * 32, 32)
    landing = weights.at[pl.ds(row, 32)]
    is_self = core == x_lo
    tile_copies = []
    for dz in (2, 1, 3, 0):
        for dx in (2, 1, 3, 0):
            xd, zd = (x + dx) % 4, (z + dz) % 4
            source = pack_ref.at[(xd // 2) * 8 + (xd % 2) * 4 + zd]
            copy = remote(
                source,
                landing,
                a_send.at[dz * 4 + dx],
                a_recv.at[z // 2],
                device(xd, y, zd, x_lo),
            )
            if (dx, dz) == (0, 0):
                local = pltpu.make_async_copy(source, landing, a_recv.at[z // 2])
                pl.when(is_self)(local.start)
                pl.when(jnp.logical_not(is_self))(copy.start)
            else:
                copy.start()
            tile_copies.append(copy)

    fold_row = pl.multiple_of(y * 256 + z * 64 + x_hi * 32 + core * 16, 16)
    fold_landing = folded.at[pl.ds(fold_row, 16)]
    for dz in (2, 1, 3, 0):
        for dx in (2, 1, 3, 0):
            copy = remote(
                fold_ref,
                fold_landing,
                f_send.at[dz * 4 + dx],
                f_recv.at[0],
                device(x + dx, y, z + dz, x_lo),
            )
            if (dx, dz) == (0, 0):
                local = pltpu.make_async_copy(fold_ref, fold_landing, f_recv.at[0])
                pl.when(is_self)(local.start)
                pl.when(jnp.logical_not(is_self))(copy.start)
            else:
                copy.start()
            tile_copies.append(copy)

    half = pl.ds(pl.multiple_of(core * 2048, 2048), 2048)
    mine = x_lo * 4 + z

    def piece(dz, h):
        return act.at[x_lo * 4 + (z + dz) % 4, pl.ds(h * 64, 64)]

    own_copy = pltpu.make_async_copy(act_ref.at[:, half], act.at[mine], own_sem)
    own_copy.start()
    started = []

    def z_go(source, target, slot, step):
        copy = remote(
            source, target, z_send.at[slot], z_recv.at[slot], device(x, y, z + step, core)
        )
        copy.start()
        started.append(copy)

    def x_go(source, target, rel, h):
        slot = rel * 2 + h
        copy = remote(
            source,
            target,
            x_send.at[slot],
            x_recv.at[slot],
            device(x + (1 if h == 0 else 3), y, z, core),
        )
        copy.start()
        started.append(copy)

    own_half = [act_ref.at[pl.ds(h * 64, 64), half] for h in range(2)]
    z_go(own_half[0], piece(0, 0), 0, 1)
    z_go(own_half[1], piece(0, 1), 3, 3)
    x_go(own_half[0], piece(0, 0), 0, 0)
    x_go(own_half[1], piece(0, 1), 0, 1)
    z_go(own_half[1], piece(0, 1), 1, 1)
    z_go(own_half[0], piece(0, 0), 2, 3)

    def block(dy, h):
        return weights.at[pl.ds(pl.multiple_of(((y + dy) % 4) * 512 + h * 256, 256), 256)]

    def y_go(dy, h, slot, step):
        copy = remote(
            block(dy, h),
            block(dy, h),
            b_send.at[slot],
            b_recv.at[slot],
            device(x, y + step, z, core),
        )
        copy.start()
        started.append(copy)

    def fold(dy, h):
        return folded.at[pl.ds(pl.multiple_of(((y + dy) % 4) * 256 + h * 128, 128), 128)]

    def f_go(dy, h, slot, step):
        copy = remote(
            fold(dy, h),
            fold(dy, h),
            g_send.at[slot],
            g_recv.at[slot],
            device(x, y + step, z, core),
        )
        copy.start()
        started.append(copy)

    arrived(block(0, 0), a_recv.at[0])
    y_go(0, 0, 0, 1)
    arrived(block(0, 1), a_recv.at[1])
    y_go(0, 1, 3, 3)
    y_go(0, 1, 1, 1)
    y_go(0, 0, 2, 3)
    arrived(folded.at[pl.ds(pl.multiple_of(y * 256, 256), 256)], f_recv.at[0])
    f_go(0, 0, 0, 1)
    f_go(0, 1, 3, 3)
    f_go(0, 1, 1, 1)
    f_go(0, 0, 2, 3)

    arrived(piece(3, 0), z_recv.at[0])
    z_go(piece(3, 0), piece(3, 0), 4, 1)
    x_go(piece(3, 0), piece(3, 0), 1, 0)
    arrived(piece(1, 1), z_recv.at[3])
    z_go(piece(1, 1), piece(1, 1), 5, 3)
    x_go(piece(1, 1), piece(1, 1), 2, 1)
    arrived(piece(3, 1), z_recv.at[1])
    x_go(piece(3, 1), piece(3, 1), 1, 1)
    arrived(piece(1, 0), z_recv.at[2])
    x_go(piece(1, 0), piece(1, 0), 2, 0)

    arrived(block(3, 0), b_recv.at[0])
    y_go(3, 0, 4, 1)
    arrived(block(1, 1), b_recv.at[3])
    y_go(1, 1, 5, 3)
    arrived(fold(3, 0), g_recv.at[0])
    f_go(3, 0, 4, 1)
    arrived(fold(1, 1), g_recv.at[3])
    f_go(1, 1, 5, 3)

    arrived(piece(2, 0), z_recv.at[4])
    x_go(piece(2, 0), piece(2, 0), 3, 0)
    arrived(piece(2, 1), z_recv.at[5])
    x_go(piece(2, 1), piece(2, 1), 3, 1)

    def other(dz, h):
        return act.at[(1 - x_lo) * 4 + (z + dz) % 4, pl.ds(h * 64, 64)]

    for rel, dz in enumerate((0, 3, 1, 2)):
        for h in range(2):
            arrived(other(dz, h), x_recv.at[rel * 2 + h])
    own_copy.wait()
    arrived(block(3, 1), b_recv.at[1])
    arrived(block(1, 0), b_recv.at[2])
    arrived(block(2, 0), b_recv.at[4])
    arrived(block(2, 1), b_recv.at[5])
    arrived(fold(3, 1), g_recv.at[1])
    arrived(fold(1, 0), g_recv.at[2])
    arrived(fold(2, 0), g_recv.at[4])
    arrived(fold(2, 1), g_recv.at[5])

    def to_twin(i):
        return remote(
            give.at[i], got.at[i], d_send.at[i], d_recv.at[i], device(x, y, z, core + 1)
        )

    def multiply(i, carry):
        product = jnp.dot(act[i], weights[...], preferred_element_type=jnp.float32)
        first, second, shared = product[:, :256], product[:, 256:512], product[:, 512:]
        keep[i, :, :256] = jnp.where(core == 0, first, second)
        keep[i, :, 256:] = shared
        give[i, :, :256] = jnp.where(core == 0, second, first)
        give[i, :, 256:] = shared
        to_twin(i).start()
        return carry

    lax.fori_loop(0, 8, multiply, 0)

    pairs = folded[...].reshape(64, 16, 128)
    step_weight = jnp.concatenate([pairs[:, :, :64], pairs[:, :, 64:]], axis=1).reshape(2048, 64)
    step_half = jnp.dot(act[mine], step_weight, preferred_element_type=jnp.float32)
    step_give[...] = jnp.concatenate([step_half, step_half], axis=1)
    step_copy = remote(
        step_give, step_got, t_sem.at[0], t_sem.at[1], device(x, y, z, core + 1)
    )
    step_copy.start()

    bc_slot = x_lo * 2 + z % 2
    has_bc = core == z // 2

    def xz_copies(i):
        source, target = rounded.at[i], xz_ref.at[mine]
        where = device(x_hi * 2 + i // 4, y, i % 4, core)
        return (
            remote(source, target, r_send.at[i], r_recv.at[mine], where),
            pltpu.make_async_copy(source, target, r_recv.at[mine]),
        )

    def bc_copies(i):
        source, target = shared_sum.at[i], bc_ref.at[bc_slot]
        where = device(x_hi * 2 + i // 4, y, i % 4, core)
        return (
            remote(source, target, c_send.at[i], c_recv.at[bc_slot], where),
            pltpu.make_async_copy(source, target, c_recv.at[bc_slot]),
        )

    def hand_out(i, carry):
        copy = to_twin(i)
        copy.wait_recv()
        total = keep[i] + got[i]
        gate = total[:, 128:256]
        rounded[i, :, :128] = total[:, :128].astype(jnp.bfloat16)
        rounded[i, :, 128:] = (gate / (1.0 + jnp.exp(-gate))).astype(jnp.bfloat16)
        shared_sum[i] = total[:, 256:]
        far, near = xz_copies(i)
        pl.when(i != mine)(far.start)
        pl.when(i == mine)(near.start)
        far, near = bc_copies(i)
        pl.when(jnp.logical_and(has_bc, i != mine))(far.start)
        pl.when(jnp.logical_and(has_bc, i == mine))(near.start)
        return carry

    lax.fori_loop(0, 8, hand_out, 0)

    def finish(i, carry):
        to_twin(i).wait_send()
        pl.when(i != mine)(xz_copies(i)[0].wait_send)
        pl.when(jnp.logical_and(has_bc, i != mine))(bc_copies(i)[0].wait_send)
        arrived(xz_ref.at[i], r_recv.at[i])
        return carry

    lax.fori_loop(0, 8, finish, 0)
    step_copy.wait()
    step_sum = step_give[...] + step_got[...]
    columns = jnp.zeros((128, 16), jnp.float32)
    for t in range(4):
        columns += jnp.where(x_hi * 2 + core == t, step_sum[:, t * 16 : t * 16 + 16], 0.0)
    step_ref[...] = columns
    for slot in range(4):
        arrived(bc_ref.at[slot], c_recv.at[slot])
    for copy in started:
        copy.wait_send()
    for n, copy in enumerate(tile_copies):
        if n % 16 == 15:
            pl.when(jnp.logical_not(is_self))(copy.wait_send)
        else:
            copy.wait_send()


def project(pack, fold, flat_in):
    dma = pltpu.SemaphoreType.DMA
    return pl.pallas_call(
        project_kernel,
        out_shape=(
            jax.ShapeDtypeStruct((8, 128, 256), jnp.bfloat16),
            jax.ShapeDtypeStruct((4, 128, 128), jnp.float32),
            jax.ShapeDtypeStruct((128, 16), jnp.float32),
        ),
        in_specs=[pl.BlockSpec(memory_space=pltpu.VMEM)] * 3,
        out_specs=(pl.BlockSpec(memory_space=pltpu.VMEM),) * 3,
        scratch_shapes=[
            pltpu.VMEM((8, 128, 2048), jnp.bfloat16),
            pltpu.VMEM((2048, 640), jnp.bfloat16),
            pltpu.VMEM((1024, 128), jnp.bfloat16),
            pltpu.VMEM((8, 128, 384), jnp.float32),
            pltpu.VMEM((8, 128, 384), jnp.float32),
            pltpu.VMEM((8, 128, 384), jnp.float32),
            pltpu.VMEM((8, 128, 256), jnp.bfloat16),
            pltpu.VMEM((8, 128, 128), jnp.float32),
            pltpu.VMEM((128, 128), jnp.float32),
            pltpu.VMEM((128, 128), jnp.float32),
            dma(()),
            dma((16,)),
            dma((1,)),
            dma((6,)),
            dma((6,)),
            dma((2,)),
            dma((16,)),
            dma((2,)),
            dma((6,)),
            dma((6,)),
            dma((6,)),
            dma((6,)),
            dma((8,)),
            dma((8,)),
            dma((8,)),
            dma((8,)),
            dma((8,)),
            dma((8,)),
            dma((8,)),
            dma((4,)),
        ],
        compiler_params=pltpu.CompilerParams(
            collective_id=0, has_side_effects=True, vmem_limit_bytes=32 << 20
        ),
        cost_estimate=pl.CostEstimate(
            flops=1024 * 2048 * 640 * 2, bytes_accessed=150 << 20, transcendentals=0
        ),
        name="project",
    )(pack, fold, flat_in)


def mixer_kernel(
    xz_ref, bc_ref, step_ref, rate_ref, bias_ref, skip_ref, gain_ref, state_ref, hidden_ref, read, late
):
    spot = pl.program_id(0)

    @pl.when(spot == 0)
    def _():
        late[0] = bc_ref[2]
        late[1] = bc_ref[3]

    for at in range(4):
        row = spot * 4 + at
        steps_of = pl.ds(row, 4, stride=32)
        c_rows = jnp.concatenate([late[0, steps_of, :], late[1, steps_of, :]], axis=1)
        upper = c_rows.astype(jnp.bfloat16)
        lower = (c_rows - upper.astype(jnp.float32)).astype(jnp.bfloat16)
        seen = lax.dot_general(
            jnp.concatenate([upper, lower], axis=0),
            state_ref[at],
            (((1,), (1,)), ((), ())),
            preferred_element_type=jnp.float32,
        )
        for t in range(4):
            read[pl.ds(t * 32 + row, 1), :] = seen[t : t + 1] + seen[t + 4 : t + 5]

    @pl.when(spot == 7)
    def _():
        raw = step_ref[...] + bias_ref[...]
        step = jnp.maximum(raw, 0.0) + jnp.log1p(jnp.exp(-jnp.abs(raw)))
        decay = jnp.exp(-jnp.exp(rate_ref[...]) * step)
        at = [slice(t * 32, t * 32 + 32) for t in range(4)]
        b = jnp.concatenate([bc_ref[0], bc_ref[1]], axis=1)
        c = jnp.concatenate([late[0], late[1]], axis=1)
        rows, total, coefs = [], None, []
        for t in range(4):
            total = decay[at[t]] if t == 0 else total * decay[at[t]]
            coefs = [member * decay[at[t]] for member in coefs] + [step[at[t]]]
            rows.append(total)
            for s in range(t + 1):
                weight = jnp.sum(b[at[s]] * c[at[t]], axis=1, keepdims=True)
                term = coefs[s] * weight
                rows.append(term + skip_ref[...] if s == t else term)
        table = jnp.concatenate(rows, axis=0)
        head = lax.broadcasted_iota(jnp.int32, (16, 1024), 0)
        channel = lax.broadcasted_iota(jnp.int32, (16, 1024), 1)
        spread = jnp.where(channel // 64 == head, 1.0, 0.0).astype(jnp.float32)
        wide = jnp.dot(
            table, spread, precision=lax.Precision.HIGHEST, preferred_element_type=jnp.float32
        )
        xs = [
            jnp.concatenate([xz_ref[j, at[t], :128] for j in range(8)], axis=1).astype(jnp.float32)
            for t in range(4)
        ]
        k = 0
        for t in range(4):
            y = wide[k * 32 : k * 32 + 32] * read[at[t], :]
            k += 1
            for s in range(t + 1):
                y += wide[k * 32 : k * 32 + 32] * xs[s]
                k += 1
            gate = jnp.concatenate([xz_ref[j, at[t], 128:] for j in range(8)], axis=1)
            gated = y * gate.astype(jnp.float32)
            inv_rms = lax.rsqrt(jnp.mean(gated * gated, axis=1, keepdims=True) + eps)
            hidden_ref[at[t], :] = (gated * inv_rms * gain_ref[...]).astype(jnp.bfloat16)


def mixer(xz, bc, step_raw, log_rate, step_bias, skip_gain, norm_gain, state):
    whole = lambda shape: pl.BlockSpec(shape, lambda i: (0,) * len(shape))
    return pl.pallas_call(
        mixer_kernel,
        grid=(8,),
        out_shape=jax.ShapeDtypeStruct((128, 1024), jnp.bfloat16),
        in_specs=[
            whole((8, 128, 256)),
            whole((4, 128, 128)),
            whole((128, 16)),
            whole((1, 16)),
            whole((1, 16)),
            whole((1, 16)),
            whole((1, 1024)),
            pl.BlockSpec((4, 1024, 256), lambda i: (i, 0, 0)),
        ],
        out_specs=whole((128, 1024)),
        scratch_shapes=[
            pltpu.VMEM((128, 1024), jnp.float32),
            pltpu.VMEM((2, 128, 128), jnp.float32),
        ],
        compiler_params=pltpu.CompilerParams(vmem_limit_bytes=32 << 20),
        cost_estimate=pl.CostEstimate(
            flops=32 * 1024 * 256 * 8, bytes_accessed=18 << 20, transcendentals=1 << 18
        ),
        name="mixer",
    )(
        xz,
        bc,
        step_raw,
        log_rate.reshape(1, 16),
        step_bias.reshape(1, 16),
        skip_gain.reshape(1, 16),
        norm_gain.reshape(1, 1024),
        state,
    )


def output_kernel(
    hidden_ref,
    out_weight_ref,
    mix_ref,
    hid,
    weights,
    keep,
    give,
    got,
    rounded,
    own_sem,
    w_send,
    w_recv,
    s1_send,
    s1_recv,
    s2_send,
    s2_recv,
    d_send,
    d_recv,
    r_send,
    r_recv,
):
    x, y, z, core = here()
    x_lo, x_hi = x % 2, x // 2
    mine = x_lo * 4 + z
    target_x = x_lo * 2 + y % 2

    barrier = pltpu.get_barrier_semaphore()

    def signal(where):
        pl.semaphore_signal(barrier, inc=1, device_id=where, device_id_type=MESH)

    self_chip = target_x == x
    for hi in range(2):
        for up in range(2):
            for dc in range(2):
                xs, ys, cs = hi * 2 + x_hi, up * 2 + x_lo, dc
                same = jnp.logical_and(
                    jnp.logical_and(xs == x, ys == y), cs == core
                )
                pl.when(jnp.logical_not(same))(lambda w=device(xs, ys, z, cs): signal(w))
    for step in (1, 2, 3):
        signal(device(x + step, y, z, core))
        signal(device(x, y, z + step, core))
    for step in range(1, 8):
        other = (mine + step) % 8
        signal(device(x_hi * 2 + other // 4, y, other % 4, core))
    signal(device(x, y, z, core + 1))
    expected = 8 + 6 + 7 + 1
    pl.semaphore_wait(barrier, expected - jnp.where(self_chip, 1, 0))

    started = []
    own_copy = pltpu.make_async_copy(hidden_ref, hid.at[x, z], own_sem)
    own_copy.start()

    def part(h, dx, dz):
        return hid.at[(x + dx) % 4, (z + dz) % 4, pl.ds(h * 64, 64)]

    turns = (1, 3, 2)

    def go(h, source, target, stage, slot, step, along_x):
        send, recv = (s1_send, s1_recv) if stage == 1 else (s2_send, s2_recv)
        where = device(x + step, y, z, core) if along_x else device(x, y, z + step, core)
        copy = remote(source, target, send.at[h, slot], recv.at[h, slot], where)
        copy.start()
        started.append(copy)

    for n, step in enumerate(turns):
        for h in range(2):
            source = hidden_ref.at[pl.ds(h * 64, 64)]
            go(h, source, part(h, 0, 0), 1, n, step, h == 1)
    for n, step in enumerate(turns):
        for h in range(2):
            source = hidden_ref.at[pl.ds(h * 64, 64)]
            go(h, source, part(h, 0, 0), 2, n, step, h == 0)

    rows = pl.ds(pl.multiple_of((y // 2) * 128 + (x_hi * 2 + core) * 32, 32), 32)
    weight_copies = []
    for dy in (1, 2, 3, 0):
        for dc in (1, 0):
            cd = (core + dc) % 2
            slot = dy * 2 + dc
            copy = remote(
                out_weight_ref.at[cd],
                weights.at[rows],
                w_send.at[slot],
                w_recv.at[0],
                device(target_x, y + dy, z, cd),
            )
            if (dy, dc) == (0, 0):
                local = pltpu.make_async_copy(
                    out_weight_ref.at[cd], weights.at[rows], w_recv.at[0]
                )
                pl.when(self_chip)(local.start)
                pl.when(jnp.logical_not(self_chip))(copy.start)
            else:
                copy.start()
            weight_copies.append(copy)

    for n, step in enumerate(turns):
        for h in range(2):
            back = (4 - step) % 4
            held = part(h, 0, back) if h == 0 else part(h, back, 0)
            arrived(held, s1_recv.at[h, n])
            for m, onward in enumerate(turns):
                go(h, held, held, 2, 3 + n * 3 + m, onward, h == 0)

    for h in range(2):
        for n, back in enumerate((0, 3, 1, 2)):
            for m, step in enumerate(turns):
                away = (4 - step) % 4
                held = part(h, away, back) if h == 0 else part(h, back, away)
                arrived(held, s2_recv.at[h, n * 3 + m])
    own_copy.wait()
    arrived(weights, w_recv.at[0])

    def to_twin(i):
        return remote(
            give.at[i], got.at[i], d_send.at[i], d_recv.at[i], device(x, y, z, core + 1)
        )

    def against(left, right):
        return lax.dot_general(
            left, right, (((1,), (1,)), ((), ())), preferred_element_type=jnp.float32
        )

    def multiply(i, carry):
        product = against(hid[i // 4, i % 4], weights[:, :1024]) + against(
            hid[2 + i // 4, i % 4], weights[:, 1024:]
        )
        first, second = product[:, :128], product[:, 128:]
        keep[i] = jnp.where(core == 0, first, second)
        give[i] = jnp.where(core == 0, second, first)
        to_twin(i).start()
        return carry

    lax.fori_loop(0, 8, multiply, 0)

    lanes = pl.ds(pl.multiple_of(mine * 128, 128), 128)

    def mix_copies(i):
        where = device(x_hi * 2 + i // 4, y, i % 4, core)
        return (
            remote(rounded.at[i], mix_ref.at[:, lanes], r_send.at[i], r_recv.at[mine], where),
            pltpu.make_async_copy(rounded.at[i], mix_ref.at[:, lanes], r_recv.at[mine]),
        )

    def hand_out(i, carry):
        to_twin(i).wait_recv()
        rounded[i] = keep[i] + got[i]
        far, near = mix_copies(i)
        pl.when(i != mine)(far.start)
        pl.when(i == mine)(near.start)
        return carry

    lax.fori_loop(0, 8, hand_out, 0)

    def finish(i, carry):
        to_twin(i).wait_send()
        pl.when(i != mine)(mix_copies(i)[0].wait_send)
        arrived(mix_ref.at[:, pl.ds(pl.multiple_of(i * 128, 128), 128)], r_recv.at[i])
        return carry

    lax.fori_loop(0, 8, finish, 0)
    for copy in started:
        copy.wait_send()
    for copy in weight_copies[:-1]:
        copy.wait_send()
    pl.when(jnp.logical_not(self_chip))(weight_copies[-1].wait_send)


def output(hidden, out_weight):
    dma = pltpu.SemaphoreType.DMA
    return pl.pallas_call(
        output_kernel,
        out_shape=jax.ShapeDtypeStruct((128, 1024), jnp.float32),
        in_specs=[pl.BlockSpec(memory_space=pltpu.VMEM)] * 2,
        out_specs=pl.BlockSpec(memory_space=pltpu.VMEM),
        scratch_shapes=[
            pltpu.VMEM((4, 4, 128, 1024), jnp.bfloat16),
            pltpu.VMEM((256, 2048), jnp.bfloat16),
            pltpu.VMEM((8, 128, 128), jnp.float32),
            pltpu.VMEM((8, 128, 128), jnp.float32),
            pltpu.VMEM((8, 128, 128), jnp.float32),
            pltpu.VMEM((8, 128, 128), jnp.float32),
            dma(()),
            dma((8,)),
            dma((1,)),
            dma((2, 3)),
            dma((2, 3)),
            dma((2, 12)),
            dma((2, 12)),
            dma((8,)),
            dma((8,)),
            dma((8,)),
            dma((8,)),
        ],
        compiler_params=pltpu.CompilerParams(
            collective_id=1, has_side_effects=True, vmem_limit_bytes=32 << 20
        ),
        cost_estimate=pl.CostEstimate(
            flops=1024 * 2048 * 256 * 2, bytes_accessed=100 << 20, transcendentals=0
        ),
        name="output",
    )(hidden, out_weight)


def shards(
    layer_in,
    lengths,
    prior_state,
    weight_x,
    weight_z,
    weight_b,
    weight_c,
    weight_step,
    weight_out,
    log_rate,
    step_bias,
    skip_gain,
    norm_gain,
):
    tensor = lax.axis_index("tensor")
    flat_in = layer_in.reshape(128, 4096)

    def by_chip(weight):
        return weight.reshape(32, 2, 2, 8, 128).transpose(1, 3, 0, 2, 4)

    def by_row(weight):
        return weight.reshape(32, 2, 4, 128).transpose(1, 2, 0, 3)

    pair = jnp.stack([by_chip(weight_x), by_chip(weight_z)], axis=4).reshape(16, 32, 512)
    shared = jnp.concatenate([by_row(weight_b), by_row(weight_c)], axis=1).reshape(16, 32, 128)
    pack = jnp.concatenate([pair, shared], axis=2)
    fold = jnp.concatenate([weight_step[:16], weight_step[16:]], axis=1)
    xz, bc, step_raw = project(pack, fold, flat_in)
    hidden = mixer(
        xz,
        bc,
        step_raw,
        log_rate,
        step_bias,
        skip_gain,
        norm_gain,
        prior_state.reshape(32, 1024, 256),
    )

    out_weight = (
        weight_out.T.reshape(32, 2, 2, 1024).transpose(2, 0, 1, 3).reshape(2, 32, 2048)
    )
    mix = output(hidden, out_weight).reshape(4, 32, 1024)
    residual = lax.dynamic_slice_in_dim(layer_in, tensor * 1024, 1024, 2).astype(jnp.float32)
    active = lengths[None, :] > jnp.arange(4, dtype=jnp.int32)[:, None]
    return jnp.where(active[:, :, None], residual + mix, residual).astype(jnp.bfloat16)


def solution(mesh):
    placed = (
        P(None, "group", None),
        P("group"),
        P("group", "tensor", None, None),
        P(("group", "tensor"), None),
        P(("group", "tensor"), None),
        P(("group", "tensor"), None),
        P(("group", "tensor"), None),
        P(("group", "tensor"), None),
        P(None, ("group", "tensor")),
        P("tensor"),
        P("tensor"),
        P("tensor"),
        P("tensor"),
    )
    return jax.shard_map(
        shards, mesh=mesh, in_specs=placed, out_specs=P(None, "group", "tensor"), check_vma=False
    )
```

time: 974 us -> 154 us (0.16)
  the two profiles are of different devices: /device:TPU:1 before, /device:TPU:46 now
where the time goes in v1:
time: 154 us
  Pallas kernels  142 us (92%)
  local copies, waits for them, and re-layouts  10.4 us (7%)
    pallas_call x1, Pallas kernels, output(): pl.pallas_call(output_kernel, out_shape=jax.ShapeDtypeStruct((128, 1024),...  79.1 us
    pallas_call x1, Pallas kernels, project(): pl.pallas_call(project_kernel, out_shape=(jax.ShapeDtypeStruct((8, 128, 2...  56.2 us
    unnamed x24, local copies, waits for them, and re-layouts  8.81 us
    pallas_call x1, Pallas kernels, mixer(): pl.pallas_call(mixer_kernel, grid=(8,), out_shape=jax.ShapeDtypeStruct((1...  7.12 us

profile of v1, /device:TPU:46, one launch (start us, length us, event | category | flops | bytes accessed | tf_op | source)
XLA Modules:
  0.0 154.1 jit_solution(566663337383572034)
XLA Ops:
  0.0 1.0 copy.29
  1.0 1.0 copy.30
  2.0 0.2 copy_bitcast_fusion.1
  2.2 0.0 copy-start.7
  2.3 0.0 copy-start.8
  2.3 0.5 copy.25
  2.8 0.2 reshape.65
  3.0 0.1 copy-done.7
  3.1 0.0 copy-start.9
  3.1 0.0 copy-start.1
  3.1 0.0 copy-done.8
  3.2 0.1 pad_maximum_fusion.pack_ref
  3.3 0.5 copy-done.9
  3.8 0.1 pad_maximum_fusion.3.fold_ref
  3.8 0.5 copy-done.1
  4.3 0.0 copy-start.2
  4.3 0.0 copy-start.3
  4.3 0.0 copy-start.4
  4.3 0.0 copy-start.5
  4.3 56.2 %project.1 = (bf16[8,128,256]{2,1,0:T(8,128)(2,1)S(1)}, f32[4,128,128]{2,1,0:T(8,128)S(1)}, f32[128,16]{1,0:T(8,128)S(1)}) custom-call(bf16[16,32,640]{2,1,0:T(8,128)(2,1)S(1)} %pad_maximum_fusion.pack_ref, bf16[16,128]{1,0:T(8,128)(2,1)S(1)} %pad_maximum_fusion.3.fold_ref, bf16[128,4096]{1,0:T(8,128)(2,1)S(1)} %bitcast.32), custom_call_target="tpu_custom_call" | custom-call | flops 2684354560 | bytes 157286400 | tf_op jit(solution)/shard_map/project/pallas_call | solution.py:343
  60.5 0.0 copy-done.2
  60.5 0.0 copy-done.3
  60.5 0.0 copy-done.4
  60.6 0.0 copy-done.5
  60.6 0.0 copy-start
  60.6 5.8 %copy-done = bf16[32,16,64,256]{3,2,1,0:T(8,128)(2,1)S(1)} copy-done((bf16[32,16,64,256]{3,2,1,0:T(8,128)(2,1)S(1)}, bf16[32,16,64,256]{3,2,1,0:T(8,128)(2,1)}, u32[]{:S(2)}) %copy-start) | copy-done | bytes 16777240
  66.3 0.0 copy-start.6
  66.3 7.1 %mixer.1.hidden_ref = bf16[128,1024]{1,0:T(8,128)(2,1)S(1)} custom-call(bf16[8,128,256]{2,1,0:T(8,128)(2,1)S(1)} %get-tuple-element.8.xz_ref, f32[4,128,128]{2,1,0:T(8,128)S(1)} %get-tuple-element.9.bc_ref, f32[128,16]{1,0:T(8,128)S(1)} %get-tuple-element.10.step_ref, f32[1,16]{1,0:T(1,128)S(1)} %bitcast.34, f32[1,16]{1,0:T(1,128)S(1)} %bitcast.35, ...), custom_call_target="tpu_custom_call" | custom-call | flops 67108864 | bytes 18874368 | tf_op jit(solution)/shard_map/mixer/pallas_call | solution.py:462
  73.5 0.0 copy-done.6
  73.5 0.2 reshape.75
  73.7 0.2 copy.36
  73.9 0.2 reshape.76.out_weight_ref
  74.1 0.0 copy-start.10
  74.1 79.1 %output.1 = f32[128,1024]{1,0:T(8,128)S(1)} custom-call(bf16[128,1024]{1,0:T(8,128)(2,1)S(1)} %mixer.1.hidden_ref, bf16[2,32,2048]{2,1,0:T(8,128)(2,1)S(1)} %reshape.76.out_weight_ref), custom_call_target="tpu_custom_call" | custom-call | flops 1073741824 | bytes 104857600 | tf_op jit(solution)/shard_map/output/pallas_call | solution.py:671
  153.2 0.0 copy-done.10
  153.2 0.9 fusion
  (7 shorter events, 0.2 us)
Async XLA Ops:
  2.2 0.8 copy-start.7
  2.3 0.8 copy-start.8
  3.1 0.7 copy-start.9
  3.1 1.2 copy-start.1
  4.3 56.2 %copy-start.2 = (f32[1024]{0:T(1024)S(1)}, f32[1024]{0:T(1024)}, u32[]{:S(2)}) copy-start(f32[1024]{0:T(1024)} %param.25) | copy-start | bytes 12292
  4.3 56.2 %copy-start.3 = (f32[16]{0:T(128)S(1)}, f32[16]{0:T(128)}, u32[]{:S(2)}) copy-start(f32[16]{0:T(128)} %param.22) | copy-start | bytes 196
  4.3 56.2 %copy-start.4 = (f32[16]{0:T(128)S(1)}, f32[16]{0:T(128)}, u32[]{:S(2)}) copy-start(f32[16]{0:T(128)} %param.23) | copy-start | bytes 196
  4.3 56.2 %copy-start.5 = (f32[16]{0:T(128)S(1)}, f32[16]{0:T(128)}, u32[]{:S(2)}) copy-start(f32[16]{0:T(128)} %param.24) | copy-start | bytes 196
  60.6 5.8 %copy-start = (bf16[32,16,64,256]{3,2,1,0:T(8,128)(2,1)S(1)}, bf16[32,16,64,256]{3,2,1,0:T(8,128)(2,1)}, u32[]{:S(2)}) copy-start(bf16[32,16,64,256]{3,2,1,0:T(8,128)(2,1)} %param.15) | copy-start | bytes 50331652
  66.3 7.1 %copy-start.6 = (bf16[4096,32]{0,1:T(8,128)(2,1)S(1)}, bf16[4096,32]{0,1:T(8,128)(2,1)}, u32[]{:S(2)}) copy-start(bf16[4096,32]{0,1:T(8,128)(2,1)} %param.21) | copy-start | bytes 786436
  74.1 79.1 %copy-start.10 = (s32[32]{0:T(128)S(1)}, s32[32]{0:T(128)}, u32[]{:S(2)}) copy-start(s32[32]{0:T(128)} %param.14) | copy-start | bytes 388

commit v2 on v0

v2 whole, which is shorter than its diff:
```python
import jax
import jax.numpy as jnp
from jax import lax
from jax.experimental import pallas as pl
from jax.experimental.pallas import tpu as pltpu
from jax.sharding import PartitionSpec as P

MESH = pl.DeviceIdType.MESH
eps = 1e-05


def here():
    group, tensor = lax.axis_index("group"), lax.axis_index("tensor")
    return (tensor // 2) * 2 + group // 16, (group // 4) % 4, group % 4, tensor % 2


def device(x, y, z, core):
    return ((x % 2) * 16 + (y % 4) * 4 + z % 4, ((x % 4) // 2) * 2 + core % 2)


def remote(source, target, send_sem, recv_sem, where):
    return pltpu.make_async_remote_copy(
        src_ref=source,
        dst_ref=target,
        send_sem=send_sem,
        recv_sem=recv_sem,
        device_id=where,
        device_id_type=MESH,
    )


def arrived(ref, sem):
    pltpu.make_async_copy(ref, ref, sem).wait()


TURNS = (1, 3, 2)


def mixer_kernel(
    pack_ref,
    act_ref,
    out_weight_ref,
    rate_ref,
    bias_ref,
    skip_ref,
    gain_ref,
    state_ref,
    mix_ref,
    act,
    landed,
    weights,
    step_weights,
    keep,
    give,
    got,
    rounded,
    shared_sum,
    xz,
    bc,
    step_give,
    step_got,
    state,
    read,
    quarter,
    out_weights,
    hid,
    out_keep,
    out_give,
    out_got,
    back,
    s_sem,
    a_send,
    a_recv,
    b_send,
    b_recv,
    z_send,
    z_recv,
    x_send,
    x_recv,
    d_send,
    d_recv,
    r_send,
    r_recv,
    c_send,
    c_recv,
    t_sem,
    q_sem,
    w_sem,
    o1_send,
    o1_recv,
    o2_send,
    o2_recv,
    h_send,
    h_recv,
    e_send,
    e_recv,
    f_sem,
):
    x, y, z, core = here()
    x_lo, x_hi = x % 2, x // 2
    mine = x_lo * 4 + z
    twin = device(x, y, z, core + 1)
    started = []

    target_x, target_y = x_lo * 2 + y % 2, y + x_hi
    stays = jnp.logical_and(target_x == x, x_hi == 0)
    k_here = (y - x_lo + 4) % 4
    source = device((k_here % 2) * 2 + x_hi, (k_here // 2) * 2 + x_lo, z, core)

    barrier = pltpu.get_barrier_semaphore()

    def signal(where):
        pl.semaphore_signal(barrier, inc=1, device_id=where, device_id_type=MESH)

    plane = [(dx, dz) for dz in (2, 1, 3, 0) for dx in (2, 1, 3, 0)]
    for dx, dz in plane[:-1]:
        signal(device(x + dx, y, z + dz, core))
    for step in TURNS:
        signal(device(x, y + step, z, core))
    signal(twin)
    pl.when(jnp.logical_not(stays))(lambda: signal(source))

    lane = lax.broadcasted_iota(jnp.int32, (256, 128), 1)
    from_lane = lax.broadcasted_iota(jnp.int32, (256, 128), 0)
    chosen = from_lane == (lane // 32) * 64 + core * 32 + lane % 32
    picker = jnp.where(chosen, 1.0, 0.0).astype(jnp.bfloat16)
    for i in range(16):
        spot = ((i % 8) // 2) * 4 + (i // 8) * 2 + i % 2
        act[mine, :, spot * 128 : spot * 128 + 128] = jnp.dot(
            act_ref[:, i * 256 : i * 256 + 256], picker, preferred_element_type=jnp.float32
        ).astype(jnp.bfloat16)

    pl.semaphore_wait(barrier, 20 - jnp.where(stays, 1, 0))

    landing = landed.at[y, x_lo * 8 + z * 2 + x_hi]
    for n, (dx, dz) in enumerate(plane):
        xd, zd = (x + dx) % 4, (z + dz) % 4
        tile = pack_ref.at[(xd // 2) * 8 + (xd % 2) * 4 + zd]
        if n == 15:
            pltpu.make_async_copy(tile, landing, a_recv.at[x_lo]).start()
        else:
            copy = remote(tile, landing, a_send.at[n], a_recv.at[x_lo], device(xd, y, zd, core))
            copy.start()
            started.append(copy)

    def piece(dz, h):
        return act.at[x_lo * 4 + (z + dz) % 4, pl.ds(h * 64, 64)]

    def z_go(dz, h, slot, step):
        copy = remote(
            piece(dz, h),
            piece(dz, h),
            z_send.at[slot],
            z_recv.at[slot],
            device(x, y, z + step, core),
        )
        copy.start()
        started.append(copy)

    def x_go(dz, h, rel):
        slot = rel * 2 + h
        copy = remote(
            piece(dz, h),
            piece(dz, h),
            x_send.at[slot],
            x_recv.at[slot],
            device(x + (1 if h == 0 else 3), y, z, core),
        )
        copy.start()
        started.append(copy)

    z_go(0, 0, 0, 1)
    z_go(0, 1, 3, 3)
    x_go(0, 0, 0)
    x_go(0, 1, 0)
    z_go(0, 1, 1, 1)
    z_go(0, 0, 2, 3)

    quarter_copy = remote(
        out_weight_ref.at[1 - core], quarter.at[core], q_sem.at[0], q_sem.at[1], twin
    )
    quarter_copy.start()
    started.append(quarter_copy)
    quarter_own = pltpu.make_async_copy(
        out_weight_ref.at[core], quarter.at[core], q_sem.at[2]
    )
    quarter_own.start()

    state_copies = [
        pltpu.make_async_copy(
            state_ref.at[pl.ds(n * 8, 8)], state.at[pl.ds(n * 8, 8)], s_sem.at[n]
        )
        for n in range(4)
    ]
    for copy in state_copies:
        copy.start()

    def block(dy, h):
        return landed.at[(y + dy) % 4, pl.ds(h * 8, 8)]

    def y_go(dy, h, slot, step):
        copy = remote(
            block(dy, h),
            block(dy, h),
            b_send.at[slot],
            b_recv.at[slot],
            device(x, y + step, z, core),
        )
        copy.start()
        started.append(copy)

    def lay_out(dy):
        at = (y + dy) % 4
        rows = pl.ds(pl.multiple_of(at * 512, 512), 512)
        for n in range(5):
            weights[rows, n * 128 : n * 128 + 128] = landed[
                at, :, n * 32 : n * 32 + 32, :
            ].reshape(512, 128)
        pairs = landed[at, :, 160:176, :]
        step_weights[rows, :] = jnp.concatenate(
            [pairs[:, :, :64], pairs[:, :, 64:]], axis=1
        ).reshape(512, 64)

    arrived(block(0, 0), a_recv.at[0])
    y_go(0, 0, 0, 1)
    arrived(block(0, 1), a_recv.at[1])
    y_go(0, 1, 3, 3)
    y_go(0, 1, 1, 1)
    y_go(0, 0, 2, 3)

    quarter_own.wait()
    arrived(quarter.at[1 - core], q_sem.at[1])
    sent_on = remote(
        quarter,
        out_weights.at[y // 2, z, x_hi],
        w_sem.at[0],
        w_sem.at[1],
        device(target_x, target_y, z, core),
    )
    kept = pltpu.make_async_copy(quarter, out_weights.at[y // 2, z, x_hi], w_sem.at[1])
    pl.when(jnp.logical_not(stays))(sent_on.start)
    pl.when(stays)(kept.start)

    arrived(piece(3, 0), z_recv.at[0])
    z_go(3, 0, 4, 1)
    x_go(3, 0, 1)
    arrived(piece(1, 1), z_recv.at[3])
    z_go(1, 1, 5, 3)
    x_go(1, 1, 2)
    lay_out(0)
    arrived(piece(3, 1), z_recv.at[1])
    x_go(3, 1, 1)
    arrived(piece(1, 0), z_recv.at[2])
    x_go(1, 0, 2)

    arrived(block(3, 0), b_recv.at[0])
    y_go(3, 0, 4, 1)
    arrived(block(1, 1), b_recv.at[3])
    y_go(1, 1, 5, 3)

    arrived(piece(2, 0), z_recv.at[4])
    x_go(2, 0, 3)
    arrived(piece(2, 1), z_recv.at[5])
    x_go(2, 1, 3)

    arrived(block(3, 1), b_recv.at[1])
    lay_out(3)
    arrived(block(1, 0), b_recv.at[2])
    lay_out(1)

    def other(dz, h):
        return act.at[(1 - x_lo) * 4 + (z + dz) % 4, pl.ds(h * 64, 64)]

    for rel, dz in enumerate((0, 3, 1, 2)):
        for h in range(2):
            arrived(other(dz, h), x_recv.at[rel * 2 + h])
    arrived(block(2, 0), b_recv.at[4])
    arrived(block(2, 1), b_recv.at[5])
    lay_out(2)

    def columns(dk, dz, h):
        k = (k_here + dk) % 4
        return out_weights.at[k // 2, (z + dz) % 4, k % 2, h]

    def o_go(h, held, stage, slot, step, along_y):
        send, recv = (o1_send, o1_recv) if stage == 1 else (o2_send, o2_recv)
        where = device(x, y + step, z, core) if along_y else device(x, y, z + step, core)
        copy = remote(held, held, send.at[h, slot], recv.at[h, slot], where)
        copy.start()
        started.append(copy)

    arrived(out_weights.at[k_here // 2, z, k_here % 2], w_sem.at[1])
    for n, step in enumerate(TURNS):
        for h in range(2):
            o_go(h, columns(0, 0, h), 1, n, step, h == 1)
    for n, step in enumerate(TURNS):
        for h in range(2):
            o_go(h, columns(0, 0, h), 2, n, step, h == 0)

    def to_twin(i):
        return remote(give.at[i], got.at[i], d_send.at[i], d_recv.at[i], twin)

    step_half = jnp.dot(act[mine], step_weights[...], preferred_element_type=jnp.float32)
    step_give[...] = jnp.concatenate([step_half, step_half], axis=1)
    step_copy = remote(step_give, step_got, t_sem.at[0], t_sem.at[1], twin)
    step_copy.start()

    def multiply(i, carry):
        product = jnp.dot(act[i], weights[...], preferred_element_type=jnp.float32)
        first, second, shared = product[:, :256], product[:, 256:512], product[:, 512:]
        keep[i, :, :256] = jnp.where(core == 0, first, second)
        keep[i, :, 256:] = shared
        give[i, :, :256] = jnp.where(core == 0, second, first)
        give[i, :, 256:] = shared
        to_twin(i).start()
        return carry

    lax.fori_loop(0, 8, multiply, 0)

    bc_slot = x_lo * 2 + z % 2
    has_bc = core == z // 2

    def owner(i):
        return device(x_hi * 2 + i // 4, y, i % 4, core)

    def xz_far(i):
        return remote(rounded.at[i], xz.at[mine], r_send.at[i], r_recv.at[mine], owner(i))

    def bc_far(i):
        return remote(
            shared_sum.at[i], bc.at[bc_slot], c_send.at[i], c_recv.at[bc_slot], owner(i)
        )

    def hand_out(i, carry):
        to_twin(i).wait_recv()
        total = keep[i] + got[i]
        gate = total[:, 128:256]
        rounded[i, :, :128] = total[:, :128].astype(jnp.bfloat16)
        rounded[i, :, 128:] = (gate / (1.0 + jnp.exp(-gate))).astype(jnp.bfloat16)
        shared_sum[i] = total[:, 256:]

        @pl.when(i != mine)
        def _():
            xz_far(i).start()
            pl.when(has_bc)(bc_far(i).start)

        @pl.when(i == mine)
        def _():
            pltpu.make_async_copy(rounded.at[i], xz.at[mine], r_recv.at[mine]).start()

            @pl.when(has_bc)
            def _():
                pltpu.make_async_copy(
                    shared_sum.at[i], bc.at[bc_slot], c_recv.at[bc_slot]
                ).start()

        return carry

    lax.fori_loop(0, 8, hand_out, 0)

    for n, step in enumerate(TURNS):
        for h in range(2):
            came = (4 - step) % 4
            held = columns(0, came, h) if h == 0 else columns(came, 0, h)
            arrived(held, o1_recv.at[h, n])
            for m, onward in enumerate(TURNS):
                o_go(h, held, 2, 3 + n * 3 + m, onward, h == 0)

    step_copy.wait()
    step_sum = step_give[...] + step_got[...]
    step_raw = jnp.zeros((128, 16), jnp.float32)
    for t in range(4):
        step_raw += jnp.where(x_hi * 2 + core == t, step_sum[:, t * 16 : t * 16 + 16], 0.0)
    raw = step_raw + bias_ref[...]
    step_size = jnp.maximum(raw, 0.0) + jnp.log1p(jnp.exp(-jnp.abs(raw)))
    decay = jnp.exp(-jnp.exp(rate_ref[...]) * step_size)

    for slot in range(4):
        arrived(bc.at[slot], c_recv.at[slot])
    for copy in state_copies:
        copy.wait()

    def look(row, carry):
        steps_of = pl.ds(row, 4, stride=32)
        c_rows = jnp.concatenate([bc[2, steps_of, :], bc[3, steps_of, :]], axis=1)
        upper = c_rows.astype(jnp.bfloat16)
        lower = (c_rows - upper.astype(jnp.float32)).astype(jnp.bfloat16)
        seen = lax.dot_general(
            jnp.concatenate([upper, lower], axis=0),
            state[row],
            (((1,), (1,)), ((), ())),
            preferred_element_type=jnp.float32,
        )
        for t in range(4):
            read[pl.ds(t * 32 + row, 1), :] = seen[t : t + 1] + seen[t + 4 : t + 5]
        return carry

    lax.fori_loop(0, 32, look, 0, unroll=4)

    at = [slice(t * 32, t * 32 + 32) for t in range(4)]
    b = jnp.concatenate([bc[0], bc[1]], axis=1)
    c = jnp.concatenate([bc[2], bc[3]], axis=1)
    rows, total, coefs = [], None, []
    for t in range(4):
        total = decay[at[t]] if t == 0 else total * decay[at[t]]
        coefs = [member * decay[at[t]] for member in coefs] + [step_size[at[t]]]
        rows.append(total)
        for s in range(t + 1):
            term = coefs[s] * jnp.sum(b[at[s]] * c[at[t]], axis=1, keepdims=True)
            rows.append(term + skip_ref[...] if s == t else term)
    table = jnp.concatenate(rows, axis=0)
    head = lax.broadcasted_iota(jnp.int32, (16, 1024), 0)
    channel = lax.broadcasted_iota(jnp.int32, (16, 1024), 1)
    spread = jnp.where(channel // 64 == head, 1.0, 0.0).astype(jnp.float32)
    wide = jnp.dot(
        table, spread, precision=lax.Precision.HIGHEST, preferred_element_type=jnp.float32
    )

    for j in range(8):
        arrived(xz.at[j], r_recv.at[j])
    xs = [
        jnp.concatenate([xz[j, at[t], :128] for j in range(8)], axis=1).astype(jnp.float32)
        for t in range(4)
    ]
    k = 0
    for t in range(4):
        seen = wide[k * 32 : k * 32 + 32] * read[at[t], :]
        k += 1
        for s in range(t + 1):
            seen += wide[k * 32 : k * 32 + 32] * xs[s]
            k += 1
        gate = jnp.concatenate([xz[j, at[t], 128:] for j in range(8)], axis=1)
        gated = seen * gate.astype(jnp.float32)
        inv_rms = lax.rsqrt(jnp.mean(gated * gated, axis=1, keepdims=True) + eps)
        hid[x, at[t], :] = (gated * inv_rms * gain_ref[...]).astype(jnp.bfloat16)
        held = hid.at[x, pl.ds(t * 32, 32)]
        for n, step in enumerate(TURNS):
            copy = remote(
                held, held, h_send.at[n, t], h_recv.at[n, t], device(x + step, y, z, core)
            )
            copy.start()
            started.append(copy)

    for h in range(2):
        for n, came in enumerate((0, 3, 1, 2)):
            for m, step in enumerate(TURNS):
                away = (4 - step) % 4
                held = columns(away, came, h) if h == 0 else columns(came, away, h)
                arrived(held, o2_recv.at[h, n * 3 + m])
    for n, step in enumerate(TURNS):
        for t in range(4):
            arrived(hid.at[(x + 4 - step) % 4, pl.ds(t * 32, 32)], h_recv.at[n, t])

    def against(left, right):
        return lax.dot_general(
            left, right, (((1,), (1,)), ((), ())), preferred_element_type=jnp.float32
        )

    def partial(which):
        held = out_weights[which].reshape(512, 2048)
        return against(hid[0:2].reshape(256, 1024), held[:, :1024]) + against(
            hid[2:4].reshape(256, 1024), held[:, 1024:]
        )

    theirs = 1 - x_lo
    out_give[...] = partial(1 - core).reshape(2, 128, 512)

    def out_twin(i):
        return remote(out_give.at[i], out_got.at[i], e_send.at[i], e_recv.at[i], twin)

    out_twin(theirs).start()
    out_twin(x_lo).start()
    out_keep[...] = partial(core).reshape(2, 128, 512)
    half = pl.ds(pl.multiple_of(x_lo * 512, 512), 512)
    out_twin(theirs).wait_recv()
    back[...] = out_keep[theirs] + out_got[theirs]
    back_copy = remote(
        back,
        mix_ref.at[:, half],
        f_sem.at[0],
        f_sem.at[1],
        device(x_hi * 2 + theirs, y, z, core),
    )
    back_copy.start()
    out_twin(x_lo).wait_recv()
    mix_ref[:, half] = out_keep[x_lo] + out_got[x_lo]

    for copy in started:
        copy.wait_send()
    pl.when(jnp.logical_not(stays))(sent_on.wait_send)

    def sent(i, carry):
        to_twin(i).wait_send()

        @pl.when(i != mine)
        def _():
            xz_far(i).wait_send()
            pl.when(has_bc)(bc_far(i).wait_send)

        return carry

    lax.fori_loop(0, 8, sent, 0)
    out_twin(0).wait_send()
    out_twin(1).wait_send()
    back_copy.wait_send()
    arrived(mix_ref.at[:, pl.ds(pl.multiple_of(theirs * 512, 512), 512)], f_sem.at[1])


def mixer(pack, flat_in, out_weight, log_rate, step_bias, skip_gain, norm_gain, state):
    dma = pltpu.SemaphoreType.DMA
    vmem = pl.BlockSpec(memory_space=pltpu.VMEM)
    bf16, f32 = jnp.bfloat16, jnp.float32
    return pl.pallas_call(
        mixer_kernel,
        out_shape=jax.ShapeDtypeStruct((128, 1024), f32),
        in_specs=[vmem] * 7 + [pl.BlockSpec(memory_space=pl.ANY)],
        out_specs=vmem,
        scratch_shapes=[
            pltpu.VMEM((8, 128, 2048), bf16),
            pltpu.VMEM((4, 16, 176, 128), bf16),
            pltpu.VMEM((2048, 640), bf16),
            pltpu.VMEM((2048, 64), bf16),
            pltpu.VMEM((8, 128, 384), f32),
            pltpu.VMEM((8, 128, 384), f32),
            pltpu.VMEM((8, 128, 384), f32),
            pltpu.VMEM((8, 128, 256), bf16),
            pltpu.VMEM((8, 128, 128), f32),
            pltpu.VMEM((8, 128, 256), bf16),
            pltpu.VMEM((4, 128, 128), f32),
            pltpu.VMEM((128, 128), f32),
            pltpu.VMEM((128, 128), f32),
            pltpu.VMEM((32, 1024, 256), bf16),
            pltpu.VMEM((128, 1024), f32),
            pltpu.VMEM((2, 32, 2048), bf16),
            pltpu.VMEM((2, 4, 2, 2, 32, 2048), bf16),
            pltpu.VMEM((4, 128, 1024), bf16),
            pltpu.VMEM((2, 128, 512), f32),
            pltpu.VMEM((2, 128, 512), f32),
            pltpu.VMEM((2, 128, 512), f32),
            pltpu.VMEM((128, 512), f32),
            dma((4,)),
            dma((15,)),
            dma((2,)),
            dma((6,)),
            dma((6,)),
            dma((6,)),
            dma((6,)),
            dma((8,)),
            dma((8,)),
            dma((8,)),
            dma((8,)),
            dma((8,)),
            dma((8,)),
            dma((8,)),
            dma((4,)),
            dma((2,)),
            dma((3,)),
            dma((2,)),
            dma((2, 3)),
            dma((2, 3)),
            dma((2, 12)),
            dma((2, 12)),
            dma((3, 4)),
            dma((3, 4)),
            dma((2,)),
            dma((2,)),
            dma((2,)),
        ],
        compiler_params=pltpu.CompilerParams(
            collective_id=0, has_side_effects=True, vmem_limit_bytes=58 << 20
        ),
        cost_estimate=pl.CostEstimate(
            flops=4 << 30, bytes_accessed=200 << 20, transcendentals=0
        ),
        name="mixer",
    )(
        pack,
        flat_in,
        out_weight,
        log_rate.reshape(1, 16),
        step_bias.reshape(1, 16),
        skip_gain.reshape(1, 16),
        norm_gain.reshape(1, 1024),
        state,
    )


def shards(
    layer_in,
    lengths,
    prior_state,
    weight_x,
    weight_z,
    weight_b,
    weight_c,
    weight_step,
    weight_out,
    log_rate,
    step_bias,
    skip_gain,
    norm_gain,
):
    tensor = lax.axis_index("tensor")
    flat_in = layer_in.reshape(128, 4096)

    def by_chip(weight):
        return weight.reshape(32, 2, 2, 8, 128).transpose(1, 3, 2, 0, 4)

    def by_row(weight):
        return weight.reshape(32, 2, 4, 128).transpose(1, 2, 0, 3)

    pair = jnp.stack([by_chip(weight_x), by_chip(weight_z)], axis=3).reshape(16, 128, 128)
    shared = jnp.concatenate([by_row(weight_b), by_row(weight_c)], axis=1).reshape(16, 32, 128)
    fold = jnp.concatenate([weight_step[:16], weight_step[16:]], axis=1)
    fold = jnp.broadcast_to(fold[None], (16, 16, 128))
    pack = jnp.concatenate([pair, shared, fold], axis=1)
    out_weight = (
        weight_out.T.reshape(32, 2, 2, 1024).transpose(2, 0, 1, 3).reshape(2, 32, 2048)
    )
    mix = mixer(
        pack,
        flat_in,
        out_weight,
        log_rate,
        step_bias,
        skip_gain,
        norm_gain,
        prior_state.reshape(32, 1024, 256),
    ).reshape(4, 32, 1024)
    residual = lax.dynamic_slice_in_dim(layer_in, tensor * 1024, 1024, 2).astype(jnp.float32)
    active = lengths[None, :] > jnp.arange(4, dtype=jnp.int32)[:, None]
    return jnp.where(active[:, :, None], residual + mix, residual).astype(jnp.bfloat16)


def solution(mesh):
    placed = (
        P(None, "group", None),
        P("group"),
        P("group", "tensor", None, None),
        P(("group", "tensor"), None),
        P(("group", "tensor"), None),
        P(("group", "tensor"), None),
        P(("group", "tensor"), None),
        P(("group", "tensor"), None),
        P(None, ("group", "tensor")),
        P("tensor"),
        P("tensor"),
        P("tensor"),
        P("tensor"),
    )
    return jax.shard_map(
        shards, mesh=mesh, in_specs=placed, out_specs=P(None, "group", "tensor"), check_vma=False
    )
```

time: 974 us -> 109 us (0.11)
  waiting for transfers between devices: 552 us -> 0 us
  matrix products: 273 us -> 0 us
  blocking collectives: 112 us -> 0 us
  Pallas kernels: 0 us -> 101 us
  between operations: 13.6 us -> 0.15 us
    all_gather x5 -> x0, waiting for transfers between devices: 430 us -> none  [the longest x1 169 us: shards(): lax.all_gather(parted[0], 'group', axis=0, tiled=True)]
    dot_general x13 -> x0, matrix products: 273 us -> none  [the longest x4 230 us: shards(): jnp.einsum('rhpn,rn->rhp', carried, c_all[position], precision=lax.Precis...]
    reduce_scatter x4 -> x0, waiting for transfers between devices: 120 us -> none  [shards(): lax.psum_scatter(partials, 'tensor', scatter_dimension=1, tiled=True)]
    pallas_call x0 -> x1, Pallas kernels: none -> 101 us  [mixer(): pl.pallas_call(mixer_kernel, out_shape=jax.ShapeDtypeStruct((128, 1024),...]
    all_gather x1 -> x0, blocking collectives: 70.2 us -> none  [shards(): lax.all_gather(parted[4], 'group', axis=0, tiled=True)]
    all_to_all x4 -> x0, blocking collectives: 41.7 us -> none  [the longest x1 11.5 us: shards(): lax.all_to_all(weight_x, 'tensor', split_axis=1, concat_axis=0, tiled=True)]
  transfers between devices with their start and end apart: 11 -> 0, of which waited for: 9 -> 0; matrix products, arithmetic and copies ran while one was open for 28% -> 0% of each run, Pallas kernels for 0% -> 0%
where the time goes in v2:
time: 109 us; the launch traced here: 108 us
  Pallas kernels  101 us (93%)
  local copies, waits for them, and re-layouts  3.87 us (4%)
  other arithmetic  3.02 us (3%)
    pallas_call x1, Pallas kernels, mixer(): pl.pallas_call(mixer_kernel, out_shape=jax.ShapeDtypeStruct((128, 1024),...  101 us
    unnamed x12, local copies, waits for them, and re-layouts  2.29 us

profile of v2, /device:TPU:1, one launch (start us, length us, event | category | flops | bytes accessed | tf_op | source)
XLA Modules:
  0.0 108.0 jit_solution(13139917125349323204)
XLA Ops:
  0.0 1.0 copy.19
  1.0 0.0 copy-start.1
  1.0 0.0 copy-start.2
  1.0 1.0 copy.20
  2.1 0.0 copy-start.3
  2.1 0.2 copy_bitcast_fusion.1
  2.3 0.0 copy-start
  2.4 0.0 copy-done.1
  2.4 0.0 copy-done.2
  2.5 0.3 copy-done.3
  2.8 0.1 pad_maximum_fusion.3
  2.9 0.9 pad_maximum_fusion.pack_ref
  3.8 0.0 copy-done
  3.8 0.2 reshape.71
  4.0 0.2 copy.26
  4.2 0.9 reshape.72.out_weight_ref
  5.0 0.0 copy-start.4
  5.0 100.9 %mixer.1 = f32[128,1024]{1,0:T(8,128)} custom-call(bf16[16,176,128]{2,1,0:T(8,128)(2,1)} %pad_maximum_fusion.pack_ref, bf16[128,4096]{1,0:T(8,128)(2,1)} %bitcast.34, bf16[2,32,2048]{2,1,0:T(8,128)(2,1)} %reshape.72.out_weight_ref, f32[1,16]{1,0:T(1,128)} %bitcast.43, f32[1,16]{1,0:T(1,128)} %bitcast.44, f32[1,16]{1,0:T(1,128)} %bitcast.45, ...), custom_call_target="tpu_custom_call" | custom-call | flops 4294967296 | bytes 209715200 | tf_op jit(solution)/shard_map/mixer/pallas_call | solution.py:513
  106.0 0.0 copy-done.4
  106.0 2.0 %fusion = bf16[4,32,1024]{2,1,0:T(8,128)(2,1)} fusion(f32[4,32,1024]{2,1,0:T(8,128)} %bitcast.32, bf16[4,32,4096]{2,1,0:T(8,128)(2,1)} %param.13, s32[]{:T(128)S(6)} %select_n.7, pred[4,32]{1,0:T(4,128)(4,1)S(1)} %iota_compare_fusion), kind=kLoop, calls=%fused_computation.2 | loop fusion | flops 524288 | bytes 1048708 | tf_op jit(solution)/shard_map/convert_element_type | solution.py:632
  (8 shorter events, 0.2 us)
Async XLA Ops:
  1.0 1.4 %copy-start.1 = (bf16[32,1024]{1,0:T(8,128)(2,1)S(1)}, bf16[32,1024]{1,0:T(8,128)(2,1)}, u32[]{:S(2)}) copy-start(bf16[32,1024]{1,0:T(8,128)(2,1)} %param.18) | copy-start | bytes 196612
  1.0 1.4 %copy-start.2 = (bf16[32,1024]{1,0:T(8,128)(2,1)S(1)}, bf16[32,1024]{1,0:T(8,128)(2,1)}, u32[]{:S(2)}) copy-start(bf16[32,1024]{1,0:T(8,128)(2,1)} %param.19) | copy-start | bytes 196612
  2.1 0.7 copy-start.3
  2.3 1.5 %copy-start = (bf16[4096,32]{0,1:T(8,128)(2,1)S(1)}, bf16[4096,32]{0,1:T(8,128)(2,1)}, u32[]{:S(2)}) copy-start(bf16[4096,32]{0,1:T(8,128)(2,1)} %param.21) | copy-start | bytes 786436
  5.0 100.9 %copy-start.4 = (s32[32]{0:T(128)S(1)}, s32[32]{0:T(128)}, u32[]{:S(2)}) copy-start(s32[32]{0:T(128)} %param.14) | copy-start | bytes 388

commit v3 on v2

v3 whole, which is shorter than its diff:
```python
import jax
import jax.numpy as jnp
from jax import lax
from jax.experimental import pallas as pl
from jax.experimental.pallas import tpu as pltpu
from jax.sharding import PartitionSpec as P

MESH = pl.DeviceIdType.MESH
eps = 1e-05


def here():
    group, tensor = lax.axis_index("group"), lax.axis_index("tensor")
    return (tensor // 2) * 2 + group // 16, (group // 4) % 4, group % 4, tensor % 2


def device(x, y, z, core):
    return ((x % 2) * 16 + (y % 4) * 4 + z % 4, ((x % 4) // 2) * 2 + core % 2)


def remote(source, target, send_sem, recv_sem, where):
    return pltpu.make_async_remote_copy(
        src_ref=source,
        dst_ref=target,
        send_sem=send_sem,
        recv_sem=recv_sem,
        device_id=where,
        device_id_type=MESH,
    )


def arrived(ref, sem):
    pltpu.make_async_copy(ref, ref, sem).wait()


TURNS = (1, 3, 2)


def mixer_kernel(
    x_ref,
    z_ref,
    b_ref,
    c_ref,
    fold_ref,
    act_ref,
    out_weight_ref,
    rate_ref,
    bias_ref,
    skip_ref,
    gain_ref,
    state_ref,
    mix_ref,
    pack,
    act,
    landed,
    weights,
    step_weights,
    keep,
    give,
    got,
    rounded,
    shared,
    shared_got,
    xz,
    bc,
    step_give,
    step_got,
    state,
    read,
    quarter,
    out_weights,
    hid,
    out_keep,
    out_give,
    out_got,
    back,
    s_sem,
    g_send,
    g_recv,
    a_send,
    a_recv,
    b_send,
    b_recv,
    z_send,
    z_recv,
    x_send,
    x_recv,
    d_send,
    d_recv,
    r_send,
    r_recv,
    c_send,
    c_recv,
    t_sem,
    q_sem,
    w_sem,
    o_send,
    o_recv,
    h_send,
    h_recv,
    e_send,
    e_recv,
    f_send,
    f_recv,
):
    x, y, z, core = here()
    x_lo, x_hi = x % 2, x // 2
    mine = x_lo * 4 + z
    twin = device(x, y, z, core + 1)
    started = []

    target_x, target_y = x_lo * 2 + y % 2, y + x_hi
    stays = jnp.logical_and(target_x == x, x_hi == 0)
    k_here = (y - x_lo + 4) % 4
    source = device((k_here % 2) * 2 + x_hi, (k_here // 2) * 2 + x_lo, z, core)

    barrier = pltpu.get_barrier_semaphore()

    def signal(where):
        pl.semaphore_signal(barrier, inc=1, device_id=where, device_id_type=MESH)

    plane = [(dx, dz) for dz in (2, 1, 3, 0) for dx in (2, 1, 3, 0)]
    for dx, dz in plane[:-1]:
        signal(device(x + dx, y, z + dz, core))
    for step in TURNS:
        signal(device(x, y + step, z, core))
    signal(twin)
    pl.when(jnp.logical_not(stays))(lambda: signal(source))

    lane = lax.broadcasted_iota(jnp.int32, (256, 128), 1)
    from_lane = lax.broadcasted_iota(jnp.int32, (256, 128), 0)
    chosen = from_lane == (lane // 32) * 64 + core * 32 + lane % 32
    picker = jnp.where(chosen, 1.0, 0.0).astype(jnp.bfloat16)
    for i in range(16):
        spot = ((i % 8) // 2) * 4 + (i // 8) * 2 + i % 2
        act[mine, :, spot * 128 : spot * 128 + 128] = jnp.dot(
            act_ref[:, i * 256 : i * 256 + 256], picker, preferred_element_type=jnp.float32
        ).astype(jnp.bfloat16)

    fold = jnp.concatenate([fold_ref[:16], fold_ref[16:]], axis=1)
    for hi in range(2):
        for j in range(8):
            to = hi * 8 + j
            for half in range(2):
                lanes = slice((hi * 16 + half * 8 + j) * 128, (hi * 16 + half * 8 + j + 1) * 128)
                pack[to, half * 64 : half * 64 + 32] = x_ref[:, lanes]
                pack[to, half * 64 + 32 : half * 64 + 64] = z_ref[:, lanes]
            lanes = slice((hi * 4 + j % 4) * 128, (hi * 4 + j % 4 + 1) * 128)
            pack[to, 128:160] = (b_ref if j < 4 else c_ref)[:, lanes]
            pack[to, 160:176] = fold
    for hi in range(2):
        quarter[core, :, hi * 1024 : hi * 1024 + 1024] = out_weight_ref[
            :, pl.ds(pl.multiple_of((hi * 2 + core) * 1024, 1024), 1024)
        ]

    pl.semaphore_wait(barrier, 20 - jnp.where(stays, 1, 0))

    parts = (pl.ds(0, 96), pl.ds(96, 80))
    landing = landed.at[y, x_lo * 8 + z * 2 + x_hi]
    for p in range(2):
        for n, (dx, dz) in enumerate(plane):
            xd, zd = (x + dx) % 4, (z + dz) % 4
            tile = pack.at[(xd // 2) * 8 + (xd % 2) * 4 + zd, parts[p]]
            to = landing.at[parts[p]]
            if n == 15:
                pltpu.make_async_copy(tile, to, a_recv.at[p]).start()
            else:
                copy = remote(tile, to, a_send.at[p, n], a_recv.at[p], device(xd, y, zd, core))
                copy.start()
                started.append(copy)

    def piece(dz, h):
        return act.at[x_lo * 4 + (z + dz) % 4, pl.ds(h * 64, 64)]

    def other(dz, h):
        return act.at[(1 - x_lo) * 4 + (z + dz) % 4, pl.ds(h * 64, 64)]

    def z_go(dz, h, slot, step, ref=piece):
        copy = remote(
            ref(dz, h),
            ref(dz, h),
            z_send.at[slot],
            z_recv.at[slot],
            device(x, y, z + step, core),
        )
        copy.start()
        started.append(copy)

    def x_go(dz, h, rel):
        slot = rel * 2 + h
        copy = remote(
            piece(dz, h),
            piece(dz, h),
            x_send.at[slot],
            x_recv.at[slot],
            device(x + (1 if h == 0 else 3), y, z, core),
        )
        copy.start()
        started.append(copy)

    z_go(0, 0, 0, 1)
    z_go(0, 1, 3, 3)
    x_go(0, 0, 0)
    x_go(0, 1, 0)
    z_go(0, 1, 1, 1)
    z_go(0, 0, 2, 3)

    for hi in range(2):
        copy = remote(
            out_weight_ref.at[:, pl.ds(pl.multiple_of((hi * 2 + 1 - core) * 1024, 1024), 1024)],
            quarter.at[core, :, pl.ds(hi * 1024, 1024)],
            q_sem.at[hi],
            q_sem.at[2 + hi],
            twin,
        )
        copy.start()
        started.append(copy)

    state_copies = [
        pltpu.make_async_copy(
            state_ref.at[pl.ds(n * 8, 8)], state.at[pl.ds(n * 8, 8)], s_sem.at[n]
        )
        for n in range(4)
    ]
    for copy in state_copies:
        copy.start()

    def block(dy, h, p):
        return landed.at[(y + dy) % 4, pl.ds(h * 8, 8), parts[p]]

    def y_go(dy, h, p, slot, step):
        copy = remote(
            block(dy, h, p),
            block(dy, h, p),
            b_send.at[p, slot],
            b_recv.at[p, slot],
            device(x, y + step, z, core),
        )
        copy.start()
        started.append(copy)

    def y_forward(p):
        arrived(block(3, 0, p), b_recv.at[p, 0])
        y_go(3, 0, p, 4, 1)
        arrived(block(1, 1, p), b_recv.at[p, 3])
        y_go(1, 1, p, 5, 3)

    def lay_out(dy):
        at = (y + dy) % 4
        rows = pl.ds(pl.multiple_of(at * 512, 512), 512)
        for n in range(5):
            weights[rows, n * 128 : n * 128 + 128] = landed[
                at, :, n * 32 : n * 32 + 32, :
            ].reshape(512, 128)
        pairs = landed[at, :, 160:176, :]
        step_weights[rows, :] = jnp.concatenate(
            [pairs[:, :, :64], pairs[:, :, 64:]], axis=1
        ).reshape(512, 64)

    for p in range(2):
        arrived(landed.at[y, :, parts[p]], a_recv.at[p])
        y_go(0, 0, p, 0, 1)
        y_go(0, 1, p, 3, 3)
        y_go(0, 1, p, 1, 1)
        y_go(0, 0, p, 2, 3)

    arrived(piece(3, 0), z_recv.at[0])
    z_go(3, 0, 4, 1)
    x_go(3, 0, 1)
    arrived(piece(1, 1), z_recv.at[3])
    z_go(1, 1, 5, 3)
    x_go(1, 1, 2)
    y_forward(0)
    arrived(piece(3, 1), z_recv.at[1])
    x_go(3, 1, 1)
    arrived(piece(1, 0), z_recv.at[2])
    x_go(1, 0, 2)
    for hi in range(2):
        arrived(quarter.at[1 - core, :, pl.ds(hi * 1024, 1024)], q_sem.at[2 + hi])
    sent_on = remote(
        quarter,
        out_weights.at[y // 2, z, x_hi],
        w_sem.at[0],
        w_sem.at[1],
        device(target_x, target_y, z, core),
    )
    kept = pltpu.make_async_copy(quarter, out_weights.at[y // 2, z, x_hi], w_sem.at[1])
    pl.when(jnp.logical_not(stays))(sent_on.start)
    pl.when(stays)(kept.start)
    lay_out(0)
    arrived(other(3, 0), x_recv.at[2])
    z_go(3, 0, 6, 1, other)
    arrived(other(1, 1), x_recv.at[5])
    z_go(1, 1, 7, 3, other)
    y_forward(1)

    arrived(block(3, 1, 0), b_recv.at[0, 1])
    arrived(block(3, 1, 1), b_recv.at[1, 1])
    lay_out(3)
    arrived(block(1, 0, 0), b_recv.at[0, 2])
    arrived(block(1, 0, 1), b_recv.at[1, 2])
    lay_out(1)
    arrived(piece(2, 0), z_recv.at[4])
    arrived(piece(2, 1), z_recv.at[5])
    arrived(other(0, 0), x_recv.at[0])
    arrived(other(0, 1), x_recv.at[1])
    arrived(other(3, 1), x_recv.at[3])
    arrived(other(1, 0), x_recv.at[4])

    def columns(dk, dz, h):
        k = (k_here + dk) % 4
        return out_weights.at[k // 2, (z + dz) % 4, k % 2, h]

    def along(h, stage):
        return (h == 1) == (stage == 1)

    def unit(h, stage, unit_at, away):
        if along(h, stage):
            return columns(away, unit_at, h)
        return columns(unit_at, away, h)

    def o_go(h, stage, unit_at, away, slot, step, part=None):
        held = unit(h, stage, unit_at, away)
        if part is not None:
            held = held.at[pl.ds(part * 16, 16)]
        where = device(x, y + step, z, core) if along(h, stage) else device(x, y, z + step, core)
        index = (stage - 1) * 8 + unit_at * (stage - 1) * 4 + h * (4 if stage == 1 else 16) + slot
        copy = remote(held, held, o_send.at[index], o_recv.at[index], where)
        copy.start()
        started.append(copy)

    def o_wait(h, stage, unit_at, away, slot, part=None):
        held = unit(h, stage, unit_at, away)
        if part is not None:
            held = held.at[pl.ds(part * 16, 16)]
        index = (stage - 1) * 8 + unit_at * (stage - 1) * 4 + h * (4 if stage == 1 else 16) + slot
        arrived(held, o_recv.at[index])

    def o_both(h, stage, unit_at):
        o_go(h, stage, unit_at, 0, 0, 1)
        o_go(h, stage, unit_at, 0, 1, 3)

    def o_forward(h, stage, unit_at):
        o_wait(h, stage, unit_at, 3, 0)
        o_go(h, stage, unit_at, 3, 2, 1, 0)
        o_wait(h, stage, unit_at, 1, 1)
        o_go(h, stage, unit_at, 1, 3, 3, 1)

    def o_last(h, stage, unit_at):
        o_wait(h, stage, unit_at, 2, 2, 0)
        o_wait(h, stage, unit_at, 2, 3, 1)

    def o_begin():
        arrived(out_weights.at[k_here // 2, z, k_here % 2], w_sem.at[1])
        for h in range(2):
            o_both(h, 1, 0)
        for h in range(2):
            o_both(h, 2, 0)

    def o_second():
        for h in range(2):
            o_forward(h, 1, 0)
            o_both(h, 2, 3)
            o_both(h, 2, 1)

    def o_third():
        for h in range(2):
            o_last(h, 1, 0)
            o_both(h, 2, 2)
        for h in range(2):
            o_forward(h, 2, 0)

    def o_fourth():
        for h in range(2):
            o_forward(h, 2, 3)
            o_forward(h, 2, 1)

    def o_fifth():
        for h in range(2):
            o_forward(h, 2, 2)

    def o_end():
        for h in range(2):
            for unit_at in range(4):
                o_last(h, 2, unit_at)

    o_begin()
    for p in range(2):
        arrived(block(2, 0, p), b_recv.at[p, 4])
        arrived(block(2, 1, p), b_recv.at[p, 5])
    lay_out(2)
    arrived(other(2, 0), z_recv.at[6])
    arrived(other(2, 1), z_recv.at[7])

    def to_twin(i):
        return remote(give.at[i], got.at[i], d_send.at[i], d_recv.at[i], twin)

    step_half = jnp.dot(act[mine], step_weights[...], preferred_element_type=jnp.float32)
    step_give[...] = jnp.concatenate([step_half, step_half], axis=1)
    step_copy = remote(step_give, step_got, t_sem.at[0], t_sem.at[1], twin)
    step_copy.start()

    bc_slot = x_lo * 2 + z % 2
    has_bc = core == z // 2

    def bc_twin(i):
        two = pl.ds(i * 2, 2)
        return remote(shared.at[two], shared_got.at[two], g_send.at[i], g_recv.at[i], twin)

    def multiply_bc(i, carry):
        two = pl.ds(i * 2, 2)
        shared[two] = jnp.dot(
            act[two].reshape(256, 2048), weights[:, 512:], preferred_element_type=jnp.float32
        ).reshape(2, 128, 128)
        pl.when(jnp.logical_not(has_bc))(bc_twin(i).start)
        return carry

    lax.fori_loop(0, 4, multiply_bc, 0)

    def multiply(i, carry):
        product = jnp.dot(act[i], weights[:, :512], preferred_element_type=jnp.float32)
        first, second = product[:, :256], product[:, 256:]
        keep[i] = jnp.where(core == 0, first, second)
        give[i] = jnp.where(core == 0, second, first)
        to_twin(i).start()
        return carry

    def owner(i):
        return device(x_hi * 2 + i // 4, y, i % 4, core)

    def xz_far(i):
        return remote(rounded.at[i], xz.at[mine], r_send.at[i], r_recv.at[mine], owner(i))

    def bc_far(i):
        return remote(shared.at[i], bc.at[bc_slot], c_send.at[i], c_recv.at[bc_slot], owner(i))

    lax.fori_loop(0, 4, multiply, 0)

    @pl.when(has_bc)
    def _():
        for i in range(4):
            two = pl.ds(i * 2, 2)
            bc_twin(i).wait_recv()
            shared[two] = shared[two] + shared_got[two]

        def hand_out_bc(i, carry):
            pl.when(i != mine)(lambda: bc_far(i).start())

            @pl.when(i == mine)
            def _():
                pltpu.make_async_copy(
                    shared.at[i], bc.at[bc_slot], c_recv.at[bc_slot]
                ).start()

            return carry

        lax.fori_loop(0, 8, hand_out_bc, 0)

    o_second()
    lax.fori_loop(4, 8, multiply, 0)

    def hand_out(i, carry):
        to_twin(i).wait_recv()
        total = keep[i] + got[i]
        gate = total[:, 128:]
        rounded[i, :, :128] = total[:, :128].astype(jnp.bfloat16)
        rounded[i, :, 128:] = (gate / (1.0 + jnp.exp(-gate))).astype(jnp.bfloat16)
        pl.when(i != mine)(lambda: xz_far(i).start())

        @pl.when(i == mine)
        def _():
            pltpu.make_async_copy(rounded.at[i], xz.at[mine], r_recv.at[mine]).start()

        return carry

    lax.fori_loop(0, 8, hand_out, 0)
    o_third()

    step_copy.wait()
    step_sum = step_give[...] + step_got[...]
    step_raw = jnp.zeros((128, 16), jnp.float32)
    for t in range(4):
        step_raw += jnp.where(x_hi * 2 + core == t, step_sum[:, t * 16 : t * 16 + 16], 0.0)
    raw = step_raw + bias_ref[...]
    step_size = jnp.maximum(raw, 0.0) + jnp.log1p(jnp.exp(-jnp.abs(raw)))
    decay = jnp.exp(-jnp.exp(rate_ref[...]) * step_size)

    for slot in range(4):
        arrived(bc.at[slot], c_recv.at[slot])
    for copy in state_copies:
        copy.wait()

    def look(row, carry):
        steps_of = pl.ds(row, 4, stride=32)
        c_rows = jnp.concatenate([bc[2, steps_of, :], bc[3, steps_of, :]], axis=1)
        upper = c_rows.astype(jnp.bfloat16)
        lower = (c_rows - upper.astype(jnp.float32)).astype(jnp.bfloat16)
        seen = lax.dot_general(
            jnp.concatenate([upper, lower], axis=0),
            state[row],
            (((1,), (1,)), ((), ())),
            preferred_element_type=jnp.float32,
        )
        for t in range(4):
            read[pl.ds(t * 32 + row, 1), :] = seen[t : t + 1] + seen[t + 4 : t + 5]
        return carry

    lax.fori_loop(0, 16, look, 0, unroll=4)
    o_fourth()
    lax.fori_loop(16, 32, look, 0, unroll=4)

    at = [slice(t * 32, t * 32 + 32) for t in range(4)]
    b = jnp.concatenate([bc[0], bc[1]], axis=1)
    c = jnp.concatenate([bc[2], bc[3]], axis=1)
    rows, total, coefs = [], None, []
    for t in range(4):
        total = decay[at[t]] if t == 0 else total * decay[at[t]]
        coefs = [member * decay[at[t]] for member in coefs] + [step_size[at[t]]]
        rows.append(total)
        for s in range(t + 1):
            term = coefs[s] * jnp.sum(b[at[s]] * c[at[t]], axis=1, keepdims=True)
            rows.append(term + skip_ref[...] if s == t else term)
    table = jnp.concatenate(rows, axis=0)
    head = lax.broadcasted_iota(jnp.int32, (16, 1024), 0)
    channel = lax.broadcasted_iota(jnp.int32, (16, 1024), 1)
    spread = jnp.where(channel // 64 == head, 1.0, 0.0).astype(jnp.float32)
    wide = jnp.dot(
        table, spread, precision=lax.Precision.HIGHEST, preferred_element_type=jnp.float32
    )

    o_fifth()
    for j in range(8):
        arrived(xz.at[j], r_recv.at[j])

    def hid_part(block, away, part=None):
        rows_of = pl.ds(block * 64, 64) if part is None else pl.ds(block * 64 + part * 32, 32)
        return hid.at[(x + away) % 4, rows_of]

    def h_go(block, away, slot, step, part=None):
        held = hid_part(block, away, part)
        copy = remote(
            held, held, h_send.at[block, slot], h_recv.at[block, slot], device(x + step, y, z, core)
        )
        copy.start()
        started.append(copy)

    def h_forward(block):
        arrived(hid_part(block, 3), h_recv.at[block, 0])
        h_go(block, 3, 2, 1, 0)
        arrived(hid_part(block, 1), h_recv.at[block, 1])
        h_go(block, 1, 3, 3, 1)

    def h_last(block):
        arrived(hid_part(block, 2, 0), h_recv.at[block, 2])
        arrived(hid_part(block, 2, 1), h_recv.at[block, 3])

    for block in range(2):
        sixteen = [slice(t * 32 + block * 16, t * 32 + block * 16 + 16) for t in range(4)]
        xs = [
            jnp.concatenate([xz[j, sixteen[t], :128] for j in range(8)], axis=1).astype(
                jnp.float32
            )
            for t in range(4)
        ]
        k = block * 16
        for t in range(4):
            seen = wide[k : k + 16] * read[sixteen[t], :]
            k += 32
            for s in range(t + 1):
                seen += wide[k : k + 16] * xs[s]
                k += 32
            gate = jnp.concatenate([xz[j, sixteen[t], 128:] for j in range(8)], axis=1)
            gated = seen * gate.astype(jnp.float32)
            inv_rms = lax.rsqrt(jnp.mean(gated * gated, axis=1, keepdims=True) + eps)
            hid[x, block * 64 + t * 16 : block * 64 + t * 16 + 16, :] = (
                gated * inv_rms * gain_ref[...]
            ).astype(jnp.bfloat16)
        h_go(block, 0, 0, 1)
        h_go(block, 0, 1, 3)

    h_forward(0)
    h_last(0)
    h_forward(1)
    o_end()

    def against(left, right):
        return lax.dot_general(
            left, right, (((1,), (1,)), ((), ())), preferred_element_type=jnp.float32
        )

    def partial(block, which):
        held = out_weights[which].reshape(512, 2048)
        rows_of = slice(block * 64, block * 64 + 64)
        product = against(hid[0:2, rows_of].reshape(128, 1024), held[:, :1024]) + against(
            hid[2:4, rows_of].reshape(128, 1024), held[:, 1024:]
        )
        return product.reshape(2, 64, 512)

    theirs = 1 - x_lo
    half = pl.ds(pl.multiple_of(x_lo * 512, 512), 512)

    def out_twin(block):
        return remote(
            out_give.at[block], out_got.at[block], e_send.at[block], e_recv.at[block], twin
        )

    def back_copy(block):
        return remote(
            back.at[block],
            mix_ref.at[:, pl.ds(block * 16, 16), half],
            f_send.at[block],
            f_recv.at[block],
            device(x_hi * 2 + theirs, y, z, core),
        )

    def give_out(block):
        out_give[block] = partial(block, 1 - core)
        out_twin(block).start()

    def join(block):
        out_twin(block).wait_recv()
        back[block] = (out_keep[block, theirs] + out_got[block, theirs]).reshape(4, 16, 512)
        back_copy(block).start()
        mix_ref[:, block * 16 : block * 16 + 16, half] = (
            out_keep[block, x_lo] + out_got[block, x_lo]
        ).reshape(4, 16, 512)

    give_out(0)
    out_keep[0] = partial(0, core)
    h_last(1)
    give_out(1)
    join(0)
    out_keep[1] = partial(1, core)
    join(1)

    for copy in started:
        copy.wait_send()
    pl.when(jnp.logical_not(stays))(sent_on.wait_send)

    def sent(i, carry):
        to_twin(i).wait_send()

        @pl.when(i != mine)
        def _():
            xz_far(i).wait_send()
            pl.when(has_bc)(bc_far(i).wait_send)

        return carry

    lax.fori_loop(0, 8, sent, 0)

    @pl.when(jnp.logical_not(has_bc))
    def _():
        for i in range(4):
            bc_twin(i).wait_send()

    for block in range(2):
        out_twin(block).wait_send()
        back_copy(block).wait_send()
        arrived(
            mix_ref.at[:, pl.ds(block * 16, 16), pl.ds(pl.multiple_of(theirs * 512, 512), 512)],
            f_recv.at[block],
        )


def mixer(weight_x, weight_z, weight_b, weight_c, weight_step, flat_in, out_weight, log_rate, step_bias, skip_gain, norm_gain, state):
    dma = pltpu.SemaphoreType.DMA
    vmem = pl.BlockSpec(memory_space=pltpu.VMEM)
    bf16, f32 = jnp.bfloat16, jnp.float32
    return pl.pallas_call(
        mixer_kernel,
        out_shape=jax.ShapeDtypeStruct((4, 32, 1024), f32),
        in_specs=[vmem] * 11 + [pl.BlockSpec(memory_space=pl.ANY)],
        out_specs=vmem,
        scratch_shapes=[
            pltpu.VMEM((16, 176, 128), bf16),
            pltpu.VMEM((8, 128, 2048), bf16),
            pltpu.VMEM((4, 16, 176, 128), bf16),
            pltpu.VMEM((2048, 640), bf16),
            pltpu.VMEM((2048, 64), bf16),
            pltpu.VMEM((8, 128, 256), f32),
            pltpu.VMEM((8, 128, 256), f32),
            pltpu.VMEM((8, 128, 256), f32),
            pltpu.VMEM((8, 128, 256), bf16),
            pltpu.VMEM((8, 128, 128), f32),
            pltpu.VMEM((8, 128, 128), f32),
            pltpu.VMEM((8, 128, 256), bf16),
            pltpu.VMEM((4, 128, 128), f32),
            pltpu.VMEM((128, 128), f32),
            pltpu.VMEM((128, 128), f32),
            pltpu.VMEM((32, 1024, 256), bf16),
            pltpu.VMEM((128, 1024), f32),
            pltpu.VMEM((2, 32, 2048), bf16),
            pltpu.VMEM((2, 4, 2, 2, 32, 2048), bf16),
            pltpu.VMEM((4, 128, 1024), bf16),
            pltpu.VMEM((2, 2, 64, 512), f32),
            pltpu.VMEM((2, 2, 64, 512), f32),
            pltpu.VMEM((2, 2, 64, 512), f32),
            pltpu.VMEM((2, 4, 16, 512), f32),
            dma((4,)),
            dma((4,)),
            dma((4,)),
            dma((2, 15)),
            dma((2,)),
            dma((2, 6)),
            dma((2, 6)),
            dma((8,)),
            dma((8,)),
            dma((6,)),
            dma((6,)),
            dma((8,)),
            dma((8,)),
            dma((8,)),
            dma((8,)),
            dma((8,)),
            dma((4,)),
            dma((2,)),
            dma((4,)),
            dma((2,)),
            dma((40,)),
            dma((40,)),
            dma((2, 4)),
            dma((2, 4)),
            dma((2,)),
            dma((2,)),
            dma((2,)),
            dma((2,)),
        ],
        compiler_params=pltpu.CompilerParams(
            collective_id=0, has_side_effects=True, vmem_limit_bytes=58 << 20
        ),
        cost_estimate=pl.CostEstimate(
            flops=4 << 30, bytes_accessed=200 << 20, transcendentals=0
        ),
        name="mixer",
    )(
        weight_x,
        weight_z,
        weight_b,
        weight_c,
        weight_step,
        flat_in,
        out_weight,
        log_rate.reshape(1, 16),
        step_bias.reshape(1, 16),
        skip_gain.reshape(1, 16),
        norm_gain.reshape(1, 1024),
        state,
    )


def shards(
    layer_in,
    lengths,
    prior_state,
    weight_x,
    weight_z,
    weight_b,
    weight_c,
    weight_step,
    weight_out,
    log_rate,
    step_bias,
    skip_gain,
    norm_gain,
):
    tensor = lax.axis_index("tensor")
    flat_in = layer_in.reshape(128, 4096)

    mix = mixer(
        weight_x,
        weight_z,
        weight_b,
        weight_c,
        weight_step,
        flat_in,
        weight_out.T,
        log_rate,
        step_bias,
        skip_gain,
        norm_gain,
        prior_state.reshape(32, 1024, 256),
    )
    residual = lax.dynamic_slice_in_dim(layer_in, tensor * 1024, 1024, 2).astype(jnp.float32)
    active = lengths[None, :] > jnp.arange(4, dtype=jnp.int32)[:, None]
    return jnp.where(active[:, :, None], residual + mix, residual).astype(jnp.bfloat16)


def solution(mesh):
    placed = (
        P(None, "group", None),
        P("group"),
        P("group", "tensor", None, None),
        P(("group", "tensor"), None),
        P(("group", "tensor"), None),
        P(("group", "tensor"), None),
        P(("group", "tensor"), None),
        P(("group", "tensor"), None),
        P(None, ("group", "tensor")),
        P("tensor"),
        P("tensor"),
        P("tensor"),
        P("tensor"),
    )
    return jax.shard_map(
        shards, mesh=mesh, in_specs=placed, out_specs=P(None, "group", "tensor"), check_vma=False
    )
```

time: 109 us -> 96.8 us (0.89)
  Pallas kernels: 101 us -> 93.9 us
  local copies, waits for them, and re-layouts: 3.87 us -> 0 us
    pallas_call x1, Pallas kernels: 101 us -> 93.9 us  [mixer(): pl.pallas_call(mixer_kernel, out_shape=jax.ShapeDtypeStruct((4, 32, 1024)...]
    unnamed x12 -> x0, local copies, waits for them, and re-layouts: 2.29 us -> none
    reshape x5 -> x0, local copies, waits for them, and re-layouts: 1.33 us -> none  [the longest x3 1.27 us: shards(): weight_out.T.reshape(32, 2, 2, 1024).transpose(2, 0, 1, 3)]
where the time goes in v3:
time: 96.8 us; the launch traced here: 96.5 us
  Pallas kernels  93.9 us (97%)
  other arithmetic  2.61 us (3%)
    pallas_call x1, Pallas kernels, mixer(): pl.pallas_call(mixer_kernel, out_shape=jax.ShapeDtypeStruct((4, 32, 1024)...  93.9 us
    convert_element_type x1, other arithmetic, shards(): jnp.where(active[:, :, None], residual + mix, residual).astype(jnp.bfloat16)  1.95 us

profile of v3, /device:TPU:1, one launch (start us, length us, event | category | flops | bytes accessed | tf_op | source)
XLA Modules:
  0.0 96.5 jit_solution(2334521201556547545)
XLA Ops:
  0.0 0.7 iota_compare_fusion
  0.7 93.9 %mixer.1 = f32[4,32,1024]{2,1,0:T(8,128)} custom-call(bf16[32,4096]{1,0:T(8,128)(2,1)} %x_ref.1, bf16[32,4096]{1,0:T(8,128)(2,1)} %z_ref.1, bf16[32,1024]{1,0:T(8,128)(2,1)} %b_ref.1, bf16[32,1024]{1,0:T(8,128)(2,1)} %c_ref.1, bf16[32,64]{1,0:T(8,128)(2,1)} %fold_ref.1, bf16[128,4096]{1,0:T(8,128)(2,1)} %bitcast.8, bf16[32,4096]{1,0:T(8,128)(2,1)} %bitcast.9, ...), custom_call_target="tpu_custom_call" | custom-call | flops 4294967296 | bytes 209715200 | tf_op jit(solution)/shard_map/mixer/pallas_call | solution.py:670
  94.6 2.0 %fusion = bf16[4,32,1024]{2,1,0:T(8,128)(2,1)} fusion(f32[4,32,1024]{2,1,0:T(8,128)} %mixer.1, bf16[4,32,4096]{2,1,0:T(8,128)(2,1)} %param.13, s32[]{:T(128)S(6)} %select_n.7, pred[4,32]{1,0:T(4,128)(4,1)S(1)} %iota_compare_fusion), kind=kLoop, calls=%fused_computation.1 | loop fusion | flops 524288 | bytes 1048708 | tf_op jit(solution)/shard_map/convert_element_type | solution.py:786

commit v4 on v3

--- a/solution.py
+++ b/solution.py
@@ -48,8 +48,9 @@
     bias_ref,
     skip_ref,
     gain_ref,
+    length_ref,
     state_ref,
-    mix_ref,
+    out_ref,
     pack,
     act,
     landed,
@@ -74,6 +75,8 @@
     out_give,
     out_got,
     back,
+    ours,
+    theirs_in,
     s_sem,
     g_send,
     g_recv,
@@ -109,10 +112,8 @@
     twin = device(x, y, z, core + 1)
     started = []
 
-    target_x, target_y = x_lo * 2 + y % 2, y + x_hi
-    stays = jnp.logical_and(target_x == x, x_hi == 0)
-    k_here = (y - x_lo + 4) % 4
-    source = device((k_here % 2) * 2 + x_hi, (k_here // 2) * 2 + x_lo, z, core)
+    target_x = x_lo * 2 + x_hi
+    stays = target_x == x
 
     barrier = pltpu.get_barrier_semaphore()
 
@@ -125,7 +126,7 @@
     for step in TURNS:
         signal(device(x, y + step, z, core))
     signal(twin)
-    pl.when(jnp.logical_not(stays))(lambda: signal(source))
+    pl.when(jnp.logical_not(stays))(lambda: signal(device(target_x, y, z, core)))
 
     lane = lax.broadcasted_iota(jnp.int32, (256, 128), 1)
     from_lane = lax.broadcasted_iota(jnp.int32, (256, 128), 0)
@@ -257,12 +258,102 @@
             [pairs[:, :, :64], pairs[:, :, 64:]], axis=1
         ).reshape(512, 64)
 
+    def columns(dk, dz, h):
+        k = (y + dk) % 4
+        return out_weights.at[k // 2, k % 2, (z + dz) % 4, h]
+
+    def along(h, stage):
+        return (h == 1) == (stage == 1)
+
+    def unit(h, stage, unit_at, away):
+        if along(h, stage):
+            return columns(away, unit_at, h)
+        return columns(unit_at, away, h)
+
+    def o_go(h, stage, unit_at, away, slot, step, part=None):
+        held = unit(h, stage, unit_at, away)
+        if part is not None:
+            held = held.at[pl.ds(part * 16, 16)]
+        where = device(x, y + step, z, core) if along(h, stage) else device(x, y, z + step, core)
+        index = (stage - 1) * 8 + unit_at * (stage - 1) * 4 + h * (4 if stage == 1 else 16) + slot
+        copy = remote(held, held, o_send.at[index], o_recv.at[index], where)
+        copy.start()
+        started.append(copy)
+
+    def o_wait(h, stage, unit_at, away, slot, part=None):
+        held = unit(h, stage, unit_at, away)
+        if part is not None:
+            held = held.at[pl.ds(part * 16, 16)]
+        index = (stage - 1) * 8 + unit_at * (stage - 1) * 4 + h * (4 if stage == 1 else 16) + slot
+        arrived(held, o_recv.at[index])
+
+    def o_both(h, stage, unit_at):
+        o_go(h, stage, unit_at, 0, 0, 1)
+        o_go(h, stage, unit_at, 0, 1, 3)
+
+    def o_forward(h, stage, unit_at):
+        o_wait(h, stage, unit_at, 3, 0)
+        o_go(h, stage, unit_at, 3, 2, 1, 0)
+        o_wait(h, stage, unit_at, 1, 1)
+        o_go(h, stage, unit_at, 1, 3, 3, 1)
+
+    def o_last(h, stage, unit_at):
+        o_wait(h, stage, unit_at, 2, 2, 0)
+        o_wait(h, stage, unit_at, 2, 3, 1)
+
+    def o_begin():
+        arrived(out_weights.at[y // 2, y % 2, z], w_sem.at[1])
+        for h in range(2):
+            o_both(h, 1, 0)
+        for h in range(2):
+            o_both(h, 2, 0)
+
+    def o_second():
+        for h in range(2):
+            o_forward(h, 1, 0)
+            o_both(h, 2, 3)
+            o_both(h, 2, 1)
+
+    def o_third():
+        for h in range(2):
+            o_last(h, 1, 0)
+            o_both(h, 2, 2)
+        for h in range(2):
+            o_forward(h, 2, 0)
+
+    def o_fourth():
+        for h in range(2):
+            o_forward(h, 2, 3)
+            o_forward(h, 2, 1)
+
+    def o_fifth():
+        for h in range(2):
+            o_forward(h, 2, 2)
+
+    def o_end():
+        for h in range(2):
+            for unit_at in range(4):
+                o_last(h, 2, unit_at)
+
     for p in range(2):
         arrived(landed.at[y, :, parts[p]], a_recv.at[p])
         y_go(0, 0, p, 0, 1)
         y_go(0, 1, p, 3, 3)
         y_go(0, 1, p, 1, 1)
         y_go(0, 0, p, 2, 3)
+
+    for hi in range(2):
+        arrived(quarter.at[1 - core, :, pl.ds(hi * 1024, 1024)], q_sem.at[2 + hi])
+    sent_on = remote(
+        quarter,
+        out_weights.at[y // 2, y % 2, z],
+        w_sem.at[0],
+        w_sem.at[1],
+        device(target_x, y, z, core),
+    )
+    kept = pltpu.make_async_copy(quarter, out_weights.at[y // 2, y % 2, z], w_sem.at[1])
+    pl.when(jnp.logical_not(stays))(sent_on.start)
+    pl.when(stays)(kept.start)
 
     arrived(piece(3, 0), z_recv.at[0])
     z_go(3, 0, 4, 1)
@@ -275,24 +366,13 @@
     x_go(3, 1, 1)
     arrived(piece(1, 0), z_recv.at[2])
     x_go(1, 0, 2)
-    for hi in range(2):
-        arrived(quarter.at[1 - core, :, pl.ds(hi * 1024, 1024)], q_sem.at[2 + hi])
-    sent_on = remote(
-        quarter,
-        out_weights.at[y // 2, z, x_hi],
-        w_sem.at[0],
-        w_sem.at[1],
-        device(target_x, target_y, z, core),
-    )
-    kept = pltpu.make_async_copy(quarter, out_weights.at[y // 2, z, x_hi], w_sem.at[1])
-    pl.when(jnp.logical_not(stays))(sent_on.start)
-    pl.when(stays)(kept.start)
     lay_out(0)
     arrived(other(3, 0), x_recv.at[2])
     z_go(3, 0, 6, 1, other)
     arrived(other(1, 1), x_recv.at[5])
     z_go(1, 1, 7, 3, other)
     y_forward(1)
+    o_begin()
 
     arrived(block(3, 1, 0), b_recv.at[0, 1])
     arrived(block(3, 1, 1), b_recv.at[1, 1])
@@ -307,84 +387,6 @@
     arrived(other(3, 1), x_recv.at[3])
     arrived(other(1, 0), x_recv.at[4])
 
-    def columns(dk, dz, h):
-        k = (k_here + dk) % 4
-        return out_weights.at[k // 2, (z + dz) % 4, k % 2, h]
-
-    def along(h, stage):
-        return (h == 1) == (stage == 1)
-
-    def unit(h, stage, unit_at, away):
-        if along(h, stage):
-            return columns(away, unit_at, h)
-        return columns(unit_at, away, h)
-
-    def o_go(h, stage, unit_at, away, slot, step, part=None):
-        held = unit(h, stage, unit_at, away)
-        if part is not None:
-            held = held.at[pl.ds(part * 16, 16)]
-        where = device(x, y + step, z, core) if along(h, stage) else device(x, y, z + step, core)
-        index = (stage - 1) * 8 + unit_at * (stage - 1) * 4 + h * (4 if stage == 1 else 16) + slot
-        copy = remote(held, held, o_send.at[index], o_recv.at[index], where)
-        copy.start()
-        started.append(copy)
-
-    def o_wait(h, stage, unit_at, away, slot, part=None):
-        held = unit(h, stage, unit_at, away)
-        if part is not None:
-            held = held.at[pl.ds(part * 16, 16)]
-        index = (stage - 1) * 8 + unit_at * (stage - 1) * 4 + h * (4 if stage == 1 else 16) + slot
-        arrived(held, o_recv.at[index])
-
-    def o_both(h, stage, unit_at):
-        o_go(h, stage, unit_at, 0, 0, 1)
-        o_go(h, stage, unit_at, 0, 1, 3)
-
-    def o_forward(h, stage, unit_at):
-        o_wait(h, stage, unit_at, 3, 0)
-        o_go(h, stage, unit_at, 3, 2, 1, 0)
-        o_wait(h, stage, unit_at, 1, 1)
-        o_go(h, stage, unit_at, 1, 3, 3, 1)
-
-    def o_last(h, stage, unit_at):
-        o_wait(h, stage, unit_at, 2, 2, 0)
-        o_wait(h, stage, unit_at, 2, 3, 1)
-
-    def o_begin():
-        arrived(out_weights.at[k_here // 2, z, k_here % 2], w_sem.at[1])
-        for h in range(2):
-            o_both(h, 1, 0)
-        for h in range(2):
-            o_both(h, 2, 0)
-
-    def o_second():
-        for h in range(2):
-            o_forward(h, 1, 0)
-            o_both(h, 2, 3)
-            o_both(h, 2, 1)
-
-    def o_third():
-        for h in range(2):
-            o_last(h, 1, 0)
-            o_both(h, 2, 2)
-        for h in range(2):
-            o_forward(h, 2, 0)
-
-    def o_fourth():
-        for h in range(2):
-            o_forward(h, 2, 3)
-            o_forward(h, 2, 1)
-
-    def o_fifth():
-        for h in range(2):
-            o_forward(h, 2, 2)
-
-    def o_end():
-        for h in range(2):
-            for unit_at in range(4):
-                o_last(h, 2, unit_at)
-
-    o_begin()
     for p in range(2):
         arrived(block(2, 0, p), b_recv.at[p, 4])
         arrived(block(2, 1, p), b_recv.at[p, 5])
@@ -435,6 +437,7 @@
         return remote(shared.at[i], bc.at[bc_slot], c_send.at[i], c_recv.at[bc_slot], owner(i))
 
     lax.fori_loop(0, 4, multiply, 0)
+    o_second()
 
     @pl.when(has_bc)
     def _():
@@ -456,7 +459,6 @@
 
         lax.fori_loop(0, 8, hand_out_bc, 0)
 
-    o_second()
     lax.fori_loop(4, 8, multiply, 0)
 
     def hand_out(i, carry):
@@ -508,6 +510,7 @@
     lax.fori_loop(0, 16, look, 0, unroll=4)
     o_fourth()
     lax.fori_loop(16, 32, look, 0, unroll=4)
+    o_fifth()
 
     at = [slice(t * 32, t * 32 + 32) for t in range(4)]
     b = jnp.concatenate([bc[0], bc[1]], axis=1)
@@ -528,7 +531,6 @@
         table, spread, precision=lax.Precision.HIGHEST, preferred_element_type=jnp.float32
     )
 
-    o_fifth()
     for j in range(8):
         arrived(xz.at[j], r_recv.at[j])
 
@@ -597,7 +599,6 @@
         return product.reshape(2, 64, 512)
 
     theirs = 1 - x_lo
-    half = pl.ds(pl.multiple_of(x_lo * 512, 512), 512)
 
     def out_twin(block):
         return remote(
@@ -607,7 +608,7 @@
     def back_copy(block):
         return remote(
             back.at[block],
-            mix_ref.at[:, pl.ds(block * 16, 16), half],
+            theirs_in.at[:, pl.ds(block * 16, 16)],
             f_send.at[block],
             f_recv.at[block],
             device(x_hi * 2 + theirs, y, z, core),
@@ -621,7 +622,7 @@
         out_twin(block).wait_recv()
         back[block] = (out_keep[block, theirs] + out_got[block, theirs]).reshape(4, 16, 512)
         back_copy(block).start()
-        mix_ref[:, block * 16 : block * 16 + 16, half] = (
+        ours[:, block * 16 : block * 16 + 16] = (
             out_keep[block, x_lo] + out_got[block, x_lo]
         ).reshape(4, 16, 512)
 
@@ -657,20 +658,32 @@
     for block in range(2):
         out_twin(block).wait_send()
         back_copy(block).wait_send()
-        arrived(
-            mix_ref.at[:, pl.ds(block * 16, 16), pl.ds(pl.multiple_of(theirs * 512, 512), 512)],
-            f_recv.at[block],
-        )
-
-
-def mixer(weight_x, weight_z, weight_b, weight_c, weight_step, flat_in, out_weight, log_rate, step_bias, skip_gain, norm_gain, state):
+        rows_of = pl.ds(block * 16, 16)
+        arrived(theirs_in.at[:, rows_of], f_recv.at[block])
+        first = jnp.where(x_lo == 0, ours[:, rows_of], theirs_in[:, rows_of])
+        second = jnp.where(x_lo == 0, theirs_in[:, rows_of], ours[:, rows_of])
+        for j in range(8):
+            span = slice(j * 64, j * 64 + 64)
+            mix = jnp.concatenate([first[:, :, span], second[:, :, span]], axis=2)
+            lanes = pl.ds(pl.multiple_of((x_hi * 2 + core) * 1024 + j * 128, 128), 128)
+            for t in range(4):
+                residual = act_ref[t * 32 + block * 16 : t * 32 + block * 16 + 16, lanes].astype(
+                    jnp.float32
+                )
+                active = length_ref[block * 16 : block * 16 + 16] > t
+                out_ref[t, rows_of, j * 128 : j * 128 + 128] = jnp.where(
+                    active, residual + mix[t], residual
+                ).astype(jnp.bfloat16)
+
+
+def mixer(weight_x, weight_z, weight_b, weight_c, weight_step, flat_in, out_weight, log_rate, step_bias, skip_gain, norm_gain, lengths, state):
     dma = pltpu.SemaphoreType.DMA
     vmem = pl.BlockSpec(memory_space=pltpu.VMEM)
     bf16, f32 = jnp.bfloat16, jnp.float32
     return pl.pallas_call(
         mixer_kernel,
-        out_shape=jax.ShapeDtypeStruct((4, 32, 1024), f32),
-        in_specs=[vmem] * 11 + [pl.BlockSpec(memory_space=pl.ANY)],
+        out_shape=jax.ShapeDtypeStruct((4, 32, 1024), bf16),
+        in_specs=[vmem] * 12 + [pl.BlockSpec(memory_space=pl.ANY)],
         out_specs=vmem,
         scratch_shapes=[
             pltpu.VMEM((16, 176, 128), bf16),
@@ -691,12 +704,14 @@
             pltpu.VMEM((32, 1024, 256), bf16),
             pltpu.VMEM((128, 1024), f32),
             pltpu.VMEM((2, 32, 2048), bf16),
-            pltpu.VMEM((2, 4, 2, 2, 32, 2048), bf16),
+            pltpu.VMEM((2, 2, 4, 2, 32, 2048), bf16),
             pltpu.VMEM((4, 128, 1024), bf16),
             pltpu.VMEM((2, 2, 64, 512), f32),
             pltpu.VMEM((2, 2, 64, 512), f32),
             pltpu.VMEM((2, 2, 64, 512), f32),
             pltpu.VMEM((2, 4, 16, 512), f32),
+            pltpu.VMEM((4, 32, 512), f32),
+            pltpu.VMEM((4, 32, 512), f32),
             dma((4,)),
             dma((4,)),
             dma((4,)),
@@ -745,6 +760,7 @@
         step_bias.reshape(1, 16),
         skip_gain.reshape(1, 16),
         norm_gain.reshape(1, 1024),
+        lengths.reshape(32, 1),
         state,
     )
 
@@ -764,10 +780,9 @@
     skip_gain,
     norm_gain,
 ):
-    tensor = lax.axis_index("tensor")
     flat_in = layer_in.reshape(128, 4096)
 
-    mix = mixer(
+    return mixer(
         weight_x,
         weight_z,
         weight_b,
@@ -779,11 +794,9 @@
         step_bias,
         skip_gain,
         norm_gain,
+        lengths,
         prior_state.reshape(32, 1024, 256),
     )
-    residual = lax.dynamic_slice_in_dim(layer_in, tensor * 1024, 1024, 2).astype(jnp.float32)
-    active = lengths[None, :] > jnp.arange(4, dtype=jnp.int32)[:, None]
-    return jnp.where(active[:, :, None], residual + mix, residual).astype(jnp.bfloat16)
 
 
 def solution(mesh):

time: 96.8 us -> 94.9 us (0.980)
  local copies, waits for them, and re-layouts: 0 us -> 3.01 us
  other arithmetic: 2.61 us -> 0 us
  Pallas kernels: 93.9 us -> 91.6 us
    pallas_call x1, Pallas kernels: 93.9 us -> 91.6 us  [mixer(): pl.pallas_call(mixer_kernel, out_shape=jax.ShapeDtypeStruct((4, 32, 1024)...]
    convert_element_type x1 -> x0, other arithmetic: 1.95 us -> none  [shards(): jnp.where(active[:, :, None], residual + mix, residual).astype(jnp.bfloat16)]
    unnamed x0 -> x1, local copies, waits for them, and re-layouts: none -> 1.67 us
    reshape x0 -> x1, local copies, waits for them, and re-layouts: none -> 1.34 us  [mixer(): lengths.reshape(32, 1)]
where the time goes in v4:
time: 94.9 us; the launch traced here: 94.6 us
  Pallas kernels  91.6 us (97%)
  local copies, waits for them, and re-layouts  3.01 us (3%)
    pallas_call x1, Pallas kernels, mixer(): pl.pallas_call(mixer_kernel, out_shape=jax.ShapeDtypeStruct((4, 32, 1024)...  91.6 us

profile of v4, /device:TPU:1, one launch (start us, length us, event | category | flops | bytes accessed | tf_op | source)
XLA Modules:
  0.0 94.6 jit_solution(6031690497535485455)
XLA Ops:
  0.0 1.3 %copy.14.length_ref = s32[32,1]{1,0:T(8,128)} copy(s32[32,1]{0,1:T(1,128)} %bitcast.15) | data formatting | bytes 256 | tf_op jit(solution)/shard_map/reshape | solution.py:763
  1.3 91.6 %mixer.1 = bf16[4,32,1024]{2,1,0:T(8,128)(2,1)} custom-call(bf16[32,4096]{1,0:T(8,128)(2,1)} %x_ref.1, bf16[32,4096]{1,0:T(8,128)(2,1)} %z_ref.1, bf16[32,1024]{1,0:T(8,128)(2,1)} %b_ref.1, bf16[32,1024]{1,0:T(8,128)(2,1)} %c_ref.1, bf16[32,64]{1,0:T(8,128)(2,1)} %fold_ref.1, bf16[128,4096]{1,0:T(8,128)(2,1)} %bitcast.9, bf16[32,4096]{1,0:T(8,128)(2,1)} %bitcast.10, ...), custom_call_target="tpu_custom_call" | custom-call | flops 4294967296 | bytes 209715200 | tf_op jit(solution)/shard_map/mixer/pallas_call | solution.py:683
  92.9 1.7 %copy.16 = bf16[4,32,1024]{2,1,0:T(8,128)(2,1)} copy(bf16[4,32,1024]{2,1,0:T(8,128)(2,1)} %mixer.1) | data formatting | bytes 524288

commit v5 on v4

--- a/solution.py
+++ b/solution.py
@@ -418,6 +418,7 @@
         return carry
 
     lax.fori_loop(0, 4, multiply_bc, 0)
+    o_second()
 
     def multiply(i, carry):
         product = jnp.dot(act[i], weights[:, :512], preferred_element_type=jnp.float32)
@@ -437,7 +438,6 @@
         return remote(shared.at[i], bc.at[bc_slot], c_send.at[i], c_recv.at[bc_slot], owner(i))
 
     lax.fori_loop(0, 4, multiply, 0)
-    o_second()
 
     @pl.when(has_bc)
     def _():
@@ -460,6 +460,7 @@
         lax.fori_loop(0, 8, hand_out_bc, 0)
 
     lax.fori_loop(4, 8, multiply, 0)
+    o_third()
 
     def hand_out(i, carry):
         to_twin(i).wait_recv()
@@ -476,7 +477,7 @@
         return carry
 
     lax.fori_loop(0, 8, hand_out, 0)
-    o_third()
+    o_fourth()
 
     step_copy.wait()
     step_sum = step_give[...] + step_got[...]
@@ -508,9 +509,8 @@
         return carry
 
     lax.fori_loop(0, 16, look, 0, unroll=4)
-    o_fourth()
+    o_fifth()
     lax.fori_loop(16, 32, look, 0, unroll=4)
-    o_fifth()
 
     at = [slice(t * 32, t * 32 + 32) for t in range(4)]
     b = jnp.concatenate([bc[0], bc[1]], axis=1)

time: 94.9 us -> 95.2 us (level)
  no operation moved by 1% of the time
where the time goes in v5:
time: 95.2 us; the launch traced here: 95 us
  Pallas kernels  92 us (97%)
  local copies, waits for them, and re-layouts  3.01 us (3%)
    pallas_call x1, Pallas kernels, mixer(): pl.pallas_call(mixer_kernel, out_shape=jax.ShapeDtypeStruct((4, 32, 1024)...  92 us

profile of v5, /device:TPU:1, one launch (start us, length us, event | category | flops | bytes accessed | tf_op | source)
XLA Modules:
  0.0 95.0 jit_solution(2674096598963066887)
XLA Ops:
  0.0 1.3 %copy.14.length_ref = s32[32,1]{1,0:T(8,128)} copy(s32[32,1]{0,1:T(1,128)} %bitcast.15) | data formatting | bytes 256 | tf_op jit(solution)/shard_map/reshape | solution.py:763
  1.3 92.0 %mixer.1 = bf16[4,32,1024]{2,1,0:T(8,128)(2,1)} custom-call(bf16[32,4096]{1,0:T(8,128)(2,1)} %x_ref.1, bf16[32,4096]{1,0:T(8,128)(2,1)} %z_ref.1, bf16[32,1024]{1,0:T(8,128)(2,1)} %b_ref.1, bf16[32,1024]{1,0:T(8,128)(2,1)} %c_ref.1, bf16[32,64]{1,0:T(8,128)(2,1)} %fold_ref.1, bf16[128,4096]{1,0:T(8,128)(2,1)} %bitcast.9, bf16[32,4096]{1,0:T(8,128)(2,1)} %bitcast.10, ...), custom_call_target="tpu_custom_call" | custom-call | flops 4294967296 | bytes 209715200 | tf_op jit(solution)/shard_map/mixer/pallas_call | solution.py:683
  93.3 1.7 %copy.16 = bf16[4,32,1024]{2,1,0:T(8,128)(2,1)} copy(bf16[4,32,1024]{2,1,0:T(8,128)(2,1)} %mixer.1) | data formatting | bytes 524288

commit v6 on v5

--- a/solution.py
+++ b/solution.py
@@ -128,16 +128,6 @@
     signal(twin)
     pl.when(jnp.logical_not(stays))(lambda: signal(device(target_x, y, z, core)))
 
-    lane = lax.broadcasted_iota(jnp.int32, (256, 128), 1)
-    from_lane = lax.broadcasted_iota(jnp.int32, (256, 128), 0)
-    chosen = from_lane == (lane // 32) * 64 + core * 32 + lane % 32
-    picker = jnp.where(chosen, 1.0, 0.0).astype(jnp.bfloat16)
-    for i in range(16):
-        spot = ((i % 8) // 2) * 4 + (i // 8) * 2 + i % 2
-        act[mine, :, spot * 128 : spot * 128 + 128] = jnp.dot(
-            act_ref[:, i * 256 : i * 256 + 256], picker, preferred_element_type=jnp.float32
-        ).astype(jnp.bfloat16)
-
     fold = jnp.concatenate([fold_ref[:16], fold_ref[16:]], axis=1)
     for hi in range(2):
         for j in range(8):
@@ -169,6 +159,16 @@
                 copy = remote(tile, to, a_send.at[p, n], a_recv.at[p], device(xd, y, zd, core))
                 copy.start()
                 started.append(copy)
+
+    lane = lax.broadcasted_iota(jnp.int32, (256, 128), 1)
+    from_lane = lax.broadcasted_iota(jnp.int32, (256, 128), 0)
+    chosen = from_lane == (lane // 32) * 64 + core * 32 + lane % 32
+    picker = jnp.where(chosen, 1.0, 0.0).astype(jnp.bfloat16)
+    for i in range(16):
+        spot = ((i % 8) // 2) * 4 + (i // 8) * 2 + i % 2
+        act[mine, :, spot * 128 : spot * 128 + 128] = jnp.dot(
+            act_ref[:, i * 256 : i * 256 + 256], picker, preferred_element_type=jnp.float32
+        ).astype(jnp.bfloat16)
 
     def piece(dz, h):
         return act.at[x_lo * 4 + (z + dz) % 4, pl.ds(h * 64, 64)]
@@ -420,7 +420,8 @@
     lax.fori_loop(0, 4, multiply_bc, 0)
     o_second()
 
-    def multiply(i, carry):
+    def multiply(turn, carry):
+        i = (mine + 1 + turn) % 8
         product = jnp.dot(act[i], weights[:, :512], preferred_element_type=jnp.float32)
         first, second = product[:, :256], product[:, 256:]
         keep[i] = jnp.where(core == 0, first, second)
@@ -446,7 +447,8 @@
             bc_twin(i).wait_recv()
             shared[two] = shared[two] + shared_got[two]
 
-        def hand_out_bc(i, carry):
+        def hand_out_bc(turn, carry):
+            i = (mine + 1 + turn) % 8
             pl.when(i != mine)(lambda: bc_far(i).start())
 
             @pl.when(i == mine)
@@ -462,7 +464,8 @@
     lax.fori_loop(4, 8, multiply, 0)
     o_third()
 
-    def hand_out(i, carry):
+    def hand_out(turn, carry):
+        i = (mine + 1 + turn) % 8
         to_twin(i).wait_recv()
         total = keep[i] + got[i]
         gate = total[:, 128:]

time: 95.2 us -> 94.9 us (level)
  no operation moved by 1% of the time
where the time goes in v6:
time: 94.9 us; the launch traced here: 94.7 us
  Pallas kernels  91.7 us (97%)
  local copies, waits for them, and re-layouts  3.01 us (3%)
    pallas_call x1, Pallas kernels, mixer(): pl.pallas_call(mixer_kernel, out_shape=jax.ShapeDtypeStruct((4, 32, 1024)...  91.7 us

profile of v6, /device:TPU:1, one launch (start us, length us, event | category | flops | bytes accessed | tf_op | source)
XLA Modules:
  0.0 94.7 jit_solution(16693151080342030704)
XLA Ops:
  0.0 1.3 %copy.14.length_ref = s32[32,1]{1,0:T(8,128)} copy(s32[32,1]{0,1:T(1,128)} %bitcast.15) | data formatting | bytes 256 | tf_op jit(solution)/shard_map/reshape | solution.py:766
  1.3 91.7 %mixer.1 = bf16[4,32,1024]{2,1,0:T(8,128)(2,1)} custom-call(bf16[32,4096]{1,0:T(8,128)(2,1)} %x_ref.1, bf16[32,4096]{1,0:T(8,128)(2,1)} %z_ref.1, bf16[32,1024]{1,0:T(8,128)(2,1)} %b_ref.1, bf16[32,1024]{1,0:T(8,128)(2,1)} %c_ref.1, bf16[32,64]{1,0:T(8,128)(2,1)} %fold_ref.1, bf16[128,4096]{1,0:T(8,128)(2,1)} %bitcast.9, bf16[32,4096]{1,0:T(8,128)(2,1)} %bitcast.10, ...), custom_call_target="tpu_custom_call" | custom-call | flops 4294967296 | bytes 209715200 | tf_op jit(solution)/shard_map/mixer/pallas_call | solution.py:686
  93.1 1.7 %copy.16 = bf16[4,32,1024]{2,1,0:T(8,128)(2,1)} copy(bf16[4,32,1024]{2,1,0:T(8,128)(2,1)} %mixer.1) | data formatting | bytes 524288
